TPU v7x, 256 devices: a whole 4x4x8 slice. The times are simulated.
256 devices in a mesh: batch: 4 (over y_hi, core), field: 64 (over z, x, y_lo).
Axes of the slice: x: 4, y: 4 (y_hi: 2, y_lo: 2; y = y_hi * 2 + y_lo), z: 8, core: 2. Of those that a mesh axis runs over, the one named last changes fastest.
Arguments:
- vectors: bfloat16 [4096, 128, 128, 8], P('batch', 'field'), may hold values from -6 to 6
- first_weight: bfloat16 [128, 64, 8, 512], P('field'), may hold values from -0.0234375 to 0.0234375
- second_weight: bfloat16 [512, 256], replicated, may hold values from -0.25 to 0.25
- out_weight: float32 [256], replicated, may hold values from -0.375 to 0.375
- upstream: float32 [4096], P('batch'), may hold values from -6 to 6
Outputs:
- logits: float32 [4096], P('batch')
- grad_vectors: float32 [4096, 128, 128, 8], P('batch', 'field')
- grad_first: float32 [128, 64, 8, 512], P('field', 'batch')
- grad_second: float32 [512, 256], replicated
- grad_out: float32 [256], replicated
All inputs are finite; a program needn't handle non-finite values.
Results may differ from a plain program's by a relative error of at most 0.0067.
Values may be sent and summed in bfloat16 or wider, within the bound.
No kernel may reach another device: no remote copies, remote signals or barrier semaphores. Data moves between devices by JAX's collectives and lax.ppermute only.
A program may use at most 128 MiB of HBM per device.

v0:
```python
import jax
import jax.numpy as jnp
from jax import lax
from jax.experimental import pallas as pl
from jax.experimental.pallas import tpu as pltpu
from jax.sharding import PartitionSpec as P

PLANE = 8
LANES = 128
TURN = 512
MIB = 1024 * 1024
CORE_PAIRS = [(0, 1), (1, 0), (2, 3), (3, 2)]
FAR_PAIRS = [(0, 2), (2, 0), (1, 3), (3, 1)]
NT = (((1,), (1,)), ((), ()))


def silu_slope(value):
    sigmoid_value = jax.nn.sigmoid(value)
    return sigmoid_value * (1.0 + value * (1.0 - sigmoid_value))


def params(mib):
    return pltpu.CompilerParams(vmem_limit_bytes=mib * MIB)


def cost(flops, moved):
    return pl.CostEstimate(flops=flops, bytes_accessed=moved, transcendentals=0)


SMEM_SPEC = pl.BlockSpec(memory_space=pltpu.SMEM)


def lane_owner(shape):
    lane = lax.broadcasted_iota(jnp.int32, shape, len(shape) - 1)
    return lane // 2, lane % 2


def own_field(owner, parity, mine):
    return jnp.where(owner <= mine, 1 - parity, parity)


def sent_field(owner, parity, mine):
    return jnp.where(owner >= mine, 1 - parity, parity)


def turn_out(chosen, planes_ref, turned_ref):
    rows, latent, lanes = chosen.shape
    planes_ref[...] = chosen.reshape(rows * latent, lanes)
    for k in range(latent):
        plane = planes_ref[pl.ds(k, rows, stride=latent), :]
        turned_ref[pl.ds(k, lanes, stride=latent), :] = plane.T


def send_part(mine_ref, vectors_ref, send_ref, planes_ref, turned_ref):
    rows, _, latent, lanes = vectors_ref.shape
    owner, parity = lane_owner((1, latent, lanes))
    field = sent_field(owner, parity, mine_ref[0])
    chosen = jnp.where(
        field == 1, vectors_ref[:, 1].astype(jnp.float32), vectors_ref[:, 0].astype(jnp.float32)
    )
    turn_out(chosen, planes_ref, turned_ref)
    send_ref[...] = turned_ref[...].astype(jnp.bfloat16).reshape(send_ref.shape)


def own_part(mine_ref, vectors_ref, own_ref, planes_ref, turned_ref):
    rows, _, latent, lanes = vectors_ref.shape
    half = lanes // 2
    owner, parity = lane_owner((1, latent, lanes))
    field = own_field(owner, parity, mine_ref[0])
    chosen = jnp.where(
        field == 1, vectors_ref[:, 1].astype(jnp.float32), vectors_ref[:, 0].astype(jnp.float32)
    )
    turn_out(chosen, planes_ref, turned_ref)
    turned = turned_ref[...].reshape(half, 2, latent, rows)
    low = lax.broadcasted_iota(jnp.int32, (half, latent, rows), 0) <= mine_ref[0]
    even, odd = turned[:, 0], turned[:, 1]
    own_ref[0] = jnp.where(low, odd, even).astype(jnp.bfloat16).reshape(half * latent, rows)
    own_ref[1] = jnp.where(low, even, odd).astype(jnp.bfloat16).reshape(half * latent, rows)


def pieces(rows):
    return [pl.ds(at, min(rows, LANES)) for at in range(0, rows, LANES)]


def send_kernel(mine_ref, vectors_ref, send_ref, *scratch):
    for piece in pieces(vectors_ref.shape[0]):
        send_part(mine_ref, vectors_ref.at[piece], send_ref.at[:, :, piece], *scratch)


def own_kernel(mine_ref, vectors_ref, own_ref, *scratch):
    for piece in pieces(vectors_ref.shape[0]):
        own_part(mine_ref, vectors_ref.at[piece], own_ref.at[:, :, piece], *scratch)


def turn_call(kernel, mine, vectors, out_shape, out_block, out_map, block):
    rows, local_fields, latent, lanes = vectors.shape
    return pl.pallas_call(
        kernel,
        grid=(rows // block,),
        in_specs=[
            SMEM_SPEC,
            pl.BlockSpec((block, local_fields, latent, lanes), lambda at: (at, 0, 0, 0)),
        ],
        out_specs=pl.BlockSpec(out_block, out_map),
        out_shape=jax.ShapeDtypeStruct(out_shape, jnp.bfloat16),
        scratch_shapes=turn_scratch(block, latent, lanes),
        compiler_params=params(60),
        cost_estimate=cost(0, vectors.size * 3),
    )(mine, vectors)


def make_send(mine, vectors):
    rows, _, latent, lanes = vectors.shape
    owners, block = lanes // 2, min(rows, TURN)
    return turn_call(
        send_kernel,
        mine,
        vectors,
        (owners, 2 * latent, rows),
        (owners, 2 * latent, block),
        lambda at: (0, 0, at),
        block,
    )


def make_own(mine, vectors):
    rows, _, latent, lanes = vectors.shape
    half, block = lanes // 2, min(rows, TURN)
    return turn_call(
        own_kernel,
        mine,
        vectors,
        (2, half * latent, rows),
        (2, half * latent, block),
        lambda at: (0, 0, at),
        block,
    )


def pairs_kernel(mine_ref, own_ref, other_ref, weights_ref, pairs_ref, partial_ref):
    half = other_ref.shape[0]
    rows = other_ref.shape[2]
    latent = own_ref.shape[1] // half
    total = None
    others = other_ref[...].astype(jnp.float32).reshape(half, 2, latent, rows)
    for i in range(2):
        own = own_ref[i].astype(jnp.float32).reshape(half, latent, rows)
        product = own * others[:, i]
        if i == 0:
            slot = lax.broadcasted_iota(jnp.int32, product.shape, 0)
            product = jnp.where(slot == mine_ref[0], 0.0, product)
        product = product.astype(jnp.bfloat16).reshape(half * latent, rows)
        pairs_ref[i] = product
        part = jnp.dot(weights_ref[i], product, preferred_element_type=jnp.float32)
        total = part if total is None else total + part
    partial_ref[...] = total.astype(jnp.bfloat16)


def make_pairs(mine, own, other, weights_turned):
    _, depth, rows = own.shape
    owners, wide, _ = other.shape
    width = weights_turned.shape[1]
    block = min(rows, 512)
    return pl.pallas_call(
        pairs_kernel,
        grid=(rows // block,),
        in_specs=[
            SMEM_SPEC,
            pl.BlockSpec((2, depth, block), lambda at: (0, 0, at)),
            pl.BlockSpec((owners, wide, block), lambda at: (0, 0, at)),
            pl.BlockSpec((2, width, depth), lambda at: (0, 0, 0)),
        ],
        out_specs=[
            pl.BlockSpec((2, depth, block), lambda at: (0, 0, at)),
            pl.BlockSpec((width, block), lambda at: (0, at)),
        ],
        out_shape=[
            jax.ShapeDtypeStruct((2, depth, rows), jnp.bfloat16),
            jax.ShapeDtypeStruct((width, rows), jnp.bfloat16),
        ],
        compiler_params=params(24),
        cost_estimate=cost(4 * depth * rows * width, 16 * depth * rows),
    )(mine, own, other, weights_turned)


def head_kernel(
    mine_ref,
    hidden_ref,
    second_ref,
    second_turned_ref,
    out_weight_ref,
    upstream_ref,
    weights_ref,
    own_ref,
    logits_ref,
    grad_second_ref,
    grad_out_ref,
    grad_hidden_ref,
    returning_ref,
):
    half = returning_ref.shape[0]
    rows = returning_ref.shape[2]
    latent = own_ref.shape[1] // half
    hidden = hidden_ref[...].astype(jnp.float32)
    sigmoid_hidden = jax.nn.sigmoid(hidden)
    activated = (hidden * sigmoid_hidden).astype(jnp.bfloat16)
    second_pre = jnp.dot(second_turned_ref[...], activated, preferred_element_type=jnp.float32)
    sigmoid_pre = jax.nn.sigmoid(second_pre)
    second_act = second_pre * sigmoid_pre
    out_weight = out_weight_ref[...]
    upstream = upstream_ref[...]
    logits_ref[...] = jnp.sum(second_act * out_weight, axis=0, keepdims=True)
    slope = sigmoid_pre * (1.0 + second_pre * (1.0 - sigmoid_pre))
    grad_pre = (upstream * out_weight * slope).astype(jnp.bfloat16)
    grad_second = lax.dot_general(activated, grad_pre, NT, preferred_element_type=jnp.float32)
    grad_out = jnp.sum(second_act * upstream, axis=1, keepdims=True)

    @pl.when(pl.program_id(0) == 0)
    def _():
        grad_second_ref[...] = grad_second
        grad_out_ref[...] = grad_out

    @pl.when(pl.program_id(0) != 0)
    def _():
        grad_second_ref[...] += grad_second
        grad_out_ref[...] += grad_out

    back_hidden = jnp.dot(second_ref[...], grad_pre, preferred_element_type=jnp.float32)
    slope = sigmoid_hidden * (1.0 + hidden * (1.0 - sigmoid_hidden))
    grad_hidden = (back_hidden * slope).astype(jnp.bfloat16)
    grad_hidden_ref[...] = grad_hidden
    returning = []
    for i in range(2):
        grads = jnp.dot(weights_ref[i], grad_hidden, preferred_element_type=jnp.float32)
        grads = grads.reshape(half, latent, rows)
        if i == 0:
            slot = lax.broadcasted_iota(jnp.int32, grads.shape, 0)
            grads = jnp.where(slot == mine_ref[0], 0.0, grads)
        own = own_ref[i].astype(jnp.float32).reshape(half, latent, rows)
        returning.append(grads * own)
    returning = jnp.stack(returning, axis=1).reshape(returning_ref.shape)
    returning_ref[...] = returning.astype(jnp.bfloat16)


def run_head(mine, hidden, second, out_weight, upstream, weights, own, latent):
    width, rows = hidden.shape
    _, depth, _ = own.shape
    owners, wide = depth // latent, 2 * latent
    width_two = second.shape[1]
    block = min(rows, 1024)
    moved = lambda at: (0, 0, at)
    fixed = lambda at: (0, 0)
    return pl.pallas_call(
        head_kernel,
        grid=(rows // block,),
        in_specs=[
            SMEM_SPEC,
            pl.BlockSpec((width, block), lambda at: (0, at)),
            pl.BlockSpec((width, width_two), fixed),
            pl.BlockSpec((width_two, width), fixed),
            pl.BlockSpec((width_two, 1), fixed),
            pl.BlockSpec((1, block), lambda at: (0, at)),
            pl.BlockSpec((2, depth, width), lambda at: (0, 0, 0)),
            pl.BlockSpec((2, depth, block), moved),
        ],
        out_specs=[
            pl.BlockSpec((1, block), lambda at: (0, at)),
            pl.BlockSpec((width, width_two), fixed),
            pl.BlockSpec((width_two, 1), fixed),
            pl.BlockSpec((width, block), lambda at: (0, at)),
            pl.BlockSpec((owners, wide, block), moved),
        ],
        out_shape=[
            jax.ShapeDtypeStruct((1, rows), jnp.float32),
            jax.ShapeDtypeStruct((width, width_two), jnp.float32),
            jax.ShapeDtypeStruct((width_two, 1), jnp.float32),
            jax.ShapeDtypeStruct((width, rows), jnp.bfloat16),
            jax.ShapeDtypeStruct((owners, wide, rows), jnp.bfloat16),
        ],
        compiler_params=params(60),
        cost_estimate=cost(4 * depth * rows * width, 24 * depth * rows),
    )(
        mine,
        hidden,
        second,
        second.T,
        out_weight.reshape(width_two, 1),
        upstream.reshape(1, rows),
        weights,
        own,
    )


def turn_back(rows, latent, lanes, turned_ref, planes_ref):
    for k in range(latent):
        plane = turned_ref[pl.ds(k, lanes, stride=latent), :]
        planes_ref[pl.ds(k, rows, stride=latent), :] = plane.T
    return planes_ref[...].reshape(rows, latent, lanes)


def own_back_part(
    mine_ref, weights_ref, grad_hidden_ref, other_ref, back_ref, planes_ref, turned_ref
):
    rows, latent, lanes = back_ref.shape
    half = lanes // 2
    shape = (half, latent, rows)
    slot = lax.broadcasted_iota(jnp.int32, shape, 0)
    low = slot <= mine_ref[0]
    others = other_ref[...].astype(jnp.float32).reshape(half, 2, latent, rows)
    grad_hidden = grad_hidden_ref[...]
    first = jnp.dot(weights_ref[0], grad_hidden, preferred_element_type=jnp.float32)
    first = jnp.where(slot == mine_ref[0], 0.0, first.reshape(shape) * others[:, 0])
    second = jnp.dot(weights_ref[1], grad_hidden, preferred_element_type=jnp.float32)
    second = second.reshape(shape) * others[:, 1]
    turned = jnp.stack([jnp.where(low, second, first), jnp.where(low, first, second)], axis=1)
    turned_ref[...] = turned.reshape(lanes * latent, rows)
    back_ref[...] = turn_back(rows, latent, lanes, turned_ref, planes_ref)


def final_part(mine_ref, back_ref, arrived_ref, grads_ref, planes_ref, turned_ref):
    rows, latent, lanes = back_ref.shape
    turned_ref[...] = arrived_ref[...].astype(jnp.float32).reshape(lanes * latent, rows)
    arrived = turn_back(rows, latent, lanes, turned_ref, planes_ref)
    owner, parity = lane_owner((1, latent, lanes))
    kept = own_field(owner, parity, mine_ref[0])
    came = sent_field(owner, parity, mine_ref[0])
    own = back_ref[...]
    for f in range(2):
        grads_ref[:, f] = jnp.where(kept == f, own, 0.0) + jnp.where(came == f, arrived, 0.0)


def own_back_kernel(mine_ref, weights_ref, grad_hidden_ref, other_ref, back_ref, *scratch):
    for piece in pieces(back_ref.shape[0]):
        own_back_part(
            mine_ref,
            weights_ref,
            grad_hidden_ref.at[:, piece],
            other_ref.at[:, :, piece],
            back_ref.at[piece],
            *scratch,
        )


def final_kernel(mine_ref, back_ref, arrived_ref, grads_ref, *scratch):
    for piece in pieces(back_ref.shape[0]):
        final_part(
            mine_ref,
            back_ref.at[piece],
            arrived_ref.at[:, :, piece],
            grads_ref.at[piece],
            *scratch,
        )


def turn_scratch(block, latent, lanes):
    block = min(block, LANES)
    return [
        pltpu.VMEM((block * latent, lanes), jnp.float32),
        pltpu.VMEM((lanes * latent, block), jnp.float32),
    ]


def turn_own_grads(mine, weights, grad_hidden, other):
    width, rows = grad_hidden.shape
    owners, wide, _ = other.shape
    latent, lanes, block = wide // 2, 2 * owners, min(rows, TURN)
    return pl.pallas_call(
        own_back_kernel,
        grid=(rows // block,),
        in_specs=[
            SMEM_SPEC,
            pl.BlockSpec(weights.shape, lambda at: (0, 0, 0)),
            pl.BlockSpec((width, block), lambda at: (0, at)),
            pl.BlockSpec((owners, wide, block), lambda at: (0, 0, at)),
        ],
        out_specs=pl.BlockSpec((block, latent, lanes), lambda at: (at, 0, 0)),
        out_shape=jax.ShapeDtypeStruct((rows, latent, lanes), jnp.float32),
        scratch_shapes=turn_scratch(block, latent, lanes),
        compiler_params=params(60),
        cost_estimate=cost(2 * weights.size * rows, other.size * 6),
    )(mine, weights, grad_hidden, other)


def join_grads(mine, back, arrived):
    rows, latent, lanes = back.shape
    owners, wide, _ = arrived.shape
    block = min(rows, TURN)
    return pl.pallas_call(
        final_kernel,
        grid=(rows // block,),
        in_specs=[
            SMEM_SPEC,
            pl.BlockSpec((block, latent, lanes), lambda at: (at, 0, 0)),
            pl.BlockSpec((owners, wide, block), lambda at: (0, 0, at)),
        ],
        out_specs=pl.BlockSpec((block, 2, latent, lanes), lambda at: (at, 0, 0, 0)),
        out_shape=jax.ShapeDtypeStruct((rows, 2, latent, lanes), jnp.float32),
        scratch_shapes=turn_scratch(block, latent, lanes),
        compiler_params=params(60),
        cost_estimate=cost(0, back.size * 14),
    )(mine, back, arrived)


def inner_groups(owners):
    return [[base + at for at in range(PLANE)] for base in range(0, owners, PLANE)]


def outer_groups(owners):
    return [[base + at for base in range(0, owners, PLANE)] for at in range(PLANE)]


def exchange(blocks, groups=None):
    return lax.all_to_all(blocks, "field", 0, 0, axis_index_groups=groups, tiled=True)


def field_sum(partial):
    owners = lax.axis_size("field")
    inner, outer = inner_groups(owners), outer_groups(owners)
    depth = owners // PLANE
    units, rows = partial.shape
    share = exchange(partial.reshape(PLANE, units // PLANE, rows), inner)
    share = jnp.sum(share.astype(jnp.float32), axis=0)
    share = exchange(share.reshape(depth, units // owners, rows), outer)
    share = jnp.sum(share, axis=0).astype(jnp.bfloat16)
    copies = jnp.broadcast_to(share[None], (depth,) + share.shape)
    plane = exchange(copies, outer).reshape(units // PLANE, rows)
    copies = jnp.broadcast_to(plane[None], (PLANE,) + plane.shape)
    return exchange(copies, inner).reshape(units, rows)


def swap(value, pairs):
    return lax.ppermute(value, "batch", pairs)


def part_of(value, index, axis):
    return lax.dynamic_index_in_dim(value, index, axis, keepdims=False)


def core_share(value, core, axis):
    return part_of(value, core, axis) + swap(part_of(value, 1 - core, axis), CORE_PAIRS)


def per_device(vectors, first_weight, second_weight, out_weight, upstream):
    local_fields, half, latent, width = first_weight.shape
    mine = lax.axis_index("field").astype(jnp.int32).reshape(1)
    turned = jnp.transpose(vectors, (0, 1, 3, 2))
    weights = first_weight.reshape(local_fields, half * latent, width)
    other = exchange(make_send(mine, turned))
    own = make_own(mine, turned)
    pairs, partial = make_pairs(mine, own, other, jnp.transpose(weights, (0, 2, 1)))
    hidden = field_sum(partial)
    logits, grad_second, grad_out, grad_hidden, returning = run_head(
        mine, hidden, second_weight, out_weight, upstream, weights, own, latent
    )
    arrived = exchange(returning)
    place = lax.axis_index("batch")
    far, core = place // 2, place % 2
    share_first = lax.dot_general(
        pairs.reshape(-1, pairs.shape[2]), grad_hidden, NT, preferred_element_type=jnp.float32
    ).reshape(local_fields, 2, 2, half // 4, latent, width)
    share_first = core_share(share_first, core, 2)
    give_first = part_of(share_first, 1 - far, 1).astype(jnp.bfloat16)
    rows_second, width_second = grad_second.shape
    share_second = core_share(grad_second.reshape(2, rows_second // 2, width_second), core, 0)
    give_first, share_second, grad_hidden = lax.optimization_barrier(
        (give_first, share_second, grad_hidden)
    )
    take_first = swap(give_first, FAR_PAIRS)
    share_second = share_second + swap(share_second, FAR_PAIRS)
    mate_second = swap(share_second, CORE_PAIRS)
    grad_out = grad_out.reshape(-1)
    grad_out = grad_out + swap(grad_out, CORE_PAIRS)
    grad_out = grad_out + swap(grad_out, FAR_PAIRS)
    back = turn_own_grads(mine, weights, grad_hidden, other)
    grad_vectors = join_grads(mine, back, arrived)
    share_first, share_second, grad_vectors = lax.optimization_barrier(
        (share_first, share_second, grad_vectors)
    )
    grad_first = part_of(share_first, far, 1) + take_first.astype(jnp.float32)
    grad_second = jnp.stack(
        [
            jnp.where(core == 0, share_second, mate_second),
            jnp.where(core == 0, mate_second, share_second),
        ]
    ).reshape(rows_second, width_second)
    grad_vectors = jnp.transpose(grad_vectors, (0, 1, 3, 2))
    return (logits.reshape(-1), grad_vectors, grad_first, grad_second, grad_out)


def solution(mesh):
    return jax.shard_map(
        per_device,
        mesh=mesh,
        in_specs=(
            P("batch", "field", None, None),
            P("field", None, None, None),
            P(),
            P(),
            P("batch"),
        ),
        out_specs=(
            P("batch"),
            P("batch", "field", None, None),
            P("field", "batch", None, None),
            P(),
            P(),
        ),
        check_vma=False,
    )
```

profile of v0, /device:TPU:16, one launch (start us, length us, event | category | flops | bytes accessed | tf_op | source)
XLA Modules:
  0.0 198.8 jit_solution(2939525266723612334)
XLA Ops:
  0.6 4.6 %shard_map.93 = bf16[64,16,1024]{2,1,0:T(8,128)(2,1)} custom-call(s32[1]{0:T(128)} %bitcast.mine_ref, bf16[1024,2,8,128]{3,2,1,0:T(8,128)(2,1)} %bitcast.41), custom_call_target="tpu_custom_call" | custom-call | bytes 6291456 | tf_op jit(solution)/shard_map/pallas_call | solution.py:97
  5.3 12.9 %all-to-all-start = ((bf16[64,16,1024]{2,1,0:T(8,128)(2,1)}), bf16[64,16,1024]{2,1,0:T(8,128)(2,1)}, u32[]{:S(2)}, u32[]{:S(2)}) async-start(bf16[64,16,1024]{2,1,0:T(8,128)(2,1)} %shard_map.93), calls=%async_computation | async-start | bytes 4194304 | tf_op jit(solution)/shard_map/all_to_all | solution.py:413
  18.2 4.6 %shard_map.92.own_ref = bf16[2,512,1024]{2,1,0:T(8,128)(2,1)} custom-call(s32[1]{0:T(128)} %bitcast.mine_ref, bf16[1024,2,8,128]{3,2,1,0:T(8,128)(2,1)} %bitcast.42), custom_call_target="tpu_custom_call" | custom-call | bytes 6291456 | tf_op jit(solution)/shard_map/pallas_call | solution.py:97
  22.8 0.0 copy-start
  22.8 1.6 copy.15.weights_ref
  24.4 44.8 %all-to-all-done.other_ref = bf16[64,16,1024]{2,1,0:T(8,128)(2,1)} async-done(((bf16[64,16,1024]{2,1,0:T(8,128)(2,1)}), bf16[64,16,1024]{2,1,0:T(8,128)(2,1)}, u32[]{:S(2)}, u32[]{:S(2)}) %all-to-all-start) | async-done | bytes 2097184 | tf_op jit(solution)/shard_map/all_to_all | solution.py:413
  69.2 0.0 copy-done
  69.2 3.0 %shard_map.94 = (bf16[2,512,1024]{2,1,0:T(8,128)(2,1)S(1)}, bf16[512,1024]{1,0:T(8,128)(2,1)S(1)}) custom-call(s32[1]{0:T(128)} %bitcast.mine_ref, bf16[2,512,1024]{2,1,0:T(8,128)(2,1)S(1)} %copy-done, bf16[64,16,1024]{2,1,0:T(8,128)(2,1)} %all-to-all-done.other_ref, bf16[2,512,512]{2,1,0:T(8,128)(2,1)S(1)} %copy.15.weights_ref), custom_call_target="tpu_custom_call" | custom-call | flops 1073741824 | bytes 8388608 | tf_op jit(solution)/shard_map/pallas_call | solution.py:164
  72.3 0.0 copy-start.1
  72.3 17.1 %all_to_all.30 = bf16[8,64,1024]{2,1,0:T(8,128)(2,1)S(1)} all-to-all(bf16[8,64,1024]{2,1,0:T(8,128)(2,1)S(1)} %bitcast.39), channel_id=1, replica_groups={{0,1,2,3,4,5,6,7},{8,9,10,11,12,13,14,15},{16,17,18,19,20,21,22,23},{24..., dimensions={0} | all-to-all | bytes 2097152 | tf_op jit(solution)/shard_map/all_to_all | solution.py:413
  89.4 0.0 copy-done.1
  89.4 0.2 convert_reduce_fusion
  89.6 14.5 %all_to_all.31 = f32[8,8,1024]{2,1,0:T(8,128)S(1)} all-to-all(f32[8,8,1024]{2,1,0:T(8,128)S(1)} %bitcast.49), channel_id=1, replica_groups={{0,8,16,24,32,40,48,56},{1,9,17,25,33,41,49,57},{2,10,18,26,34,42,50,58..., dimensions={0} | all-to-all | bytes 524288 | tf_op jit(solution)/shard_map/all_to_all | solution.py:413
  104.0 0.0 copy-start.6
  104.0 0.0 copy-start.9
  104.1 11.6 %all_to_all.32 = bf16[8,8,1024]{2,1,0:T(8,128)(2,1)S(1)} all-to-all(bf16[8,8,1024]{2,1,0:T(8,128)(2,1)S(1)} %broadcast_in_dim.6), channel_id=1, replica_groups={{0,8,16,24,32,40,48,56},{1,9,17,25,33,41,49,57},{2,10,18,26,34,42,50,58..., dimensions={0} | all-to-all | bytes 262144 | tf_op jit(solution)/shard_map/all_to_all | solution.py:413
  115.7 1.1 broadcast_in_dim.15
  116.8 3.6 %all-to-all-start.4 = ((bf16[8,64,1024]{2,1,0:T(8,128)(2,1)}), bf16[8,64,1024]{2,1,0:T(8,128)(2,1)S(1)}, u32[]{:S(2)}, u32[]{:S(2)}) async-start(bf16[8,64,1024]{2,1,0:T(8,128)(2,1)} %broadcast_in_dim.15), calls=%async_computation.4 | async-start | bytes 2097152 | tf_op jit(solution)/shard_map/all_to_all | solution.py:413
  120.3 0.0 copy-done.6
  120.3 0.8 copy.16
  121.2 0.0 copy-done.9
  121.2 0.8 copy.17.out_weight_ref
  122.0 9.7 %all-to-all-done.4 = bf16[8,64,1024]{2,1,0:T(8,128)(2,1)S(1)} async-done(((bf16[8,64,1024]{2,1,0:T(8,128)(2,1)}), bf16[8,64,1024]{2,1,0:T(8,128)(2,1)S(1)}, u32[]{:S(2)}, u32[]{:S(2)}) %all-to-all-start.4) | async-done | bytes 1048608 | tf_op jit(solution)/shard_map/all_to_all | solution.py:413
  131.6 0.0 copy-start.3
  131.6 1.0 copy-done.3
  132.6 6.4 %shard_map.95 = (f32[1,1024]{1,0:T(1,128)}, f32[512,256]{1,0:T(8,128)}, f32[256,1]{1,0:T(8,128)}, bf16[512,1024]{1,0:T(8,128)(2,1)}, bf16[64,16,1024]{2,1,0:T(8,128)(2,1)}) custom-call(s32[1]{0:T(128)} %bitcast.mine_ref, bf16[512,1024]{1,0:T(8,128)(2,1)} %bitcast.47, bf16[512,256]{1,0:T(8,128)(2,1)} %second_ref.1, bf16[256,512]{1,0:T(8,128)(2,1)} %bitcast.48, ...), custom_call_target="tpu_custom_call" | custom-call | flops 1073741824 | bytes 12582912 | tf_op jit(solution)/shard_map/pallas_call | solution.py:253
  139.0 0.0 copy-start.2
  139.0 0.0 copy-start.5
  139.0 5.8 %all-to-all-start.5 = ((bf16[64,16,1024]{2,1,0:T(8,128)(2,1)}), bf16[64,16,1024]{2,1,0:T(8,128)(2,1)}, u32[]{:S(2)}, u32[]{:S(2)}) async-start(bf16[64,16,1024]{2,1,0:T(8,128)(2,1)} %get-tuple-element.25), calls=%async_computation.5 | async-start | bytes 4194304 | tf_op jit(solution)/shard_map/all_to_all | solution.py:413
  144.9 0.0 copy-done.2
  144.9 0.0 copy-done.5
  144.9 1.3 fusion
  146.2 0.0 copy-start.4
  146.2 1.3 copy-done.4
  147.5 0.0 copy-start.7
  147.5 0.1 dynamic-slice_bitcast_fusion
  147.6 0.1 collective-permute-start
  147.7 0.9 copy-done.7
  148.6 0.1 collective-permute-start.1
  148.7 2.0 %collective-permute-done.1 = f32[256,256]{1,0:T(8,128)S(1)} collective-permute-done((f32[256,256]{1,0:T(8,128)S(1)}, f32[256,256]{1,0:T(8,128)S(1)}, u32[]{:S(2)}, u32[]{:S(2)}) %collective-permute-start.1) | collective-permute-done | bytes 262176 | tf_op jit(solution)/shard_map/ppermute | solution.py:432
  150.8 0.0 copy-start.8
  150.8 0.0 collective-permute-done
  150.8 1.5 bitcast_add_fusion
  152.3 0.9 collective-permute-start.2
  153.2 13.5 %collective-permute-done.2 = f32[256,256]{1,0:T(8,128)S(1)} collective-permute-done((f32[256,256]{1,0:T(8,128)S(1)}, f32[256,256]{1,0:T(8,128)S(1)}, u32[]{:S(2)}, u32[]{:S(2)}) %collective-permute-start.2) | collective-permute-done | bytes 262176 | tf_op jit(solution)/shard_map/ppermute | solution.py:432
  166.8 0.1 collective-permute-start.4
  166.9 0.0 copy-done.8
  166.9 0.1 reduce
  167.0 0.6 collective-permute-start.5
  167.5 0.8 collective-permute-done.5
  168.4 0.0 collective-permute-start.6
  168.4 5.1 %collective-permute-done.6 = f32[256]{0:T(256)S(1)} collective-permute-done((f32[256]{0:T(256)S(1)}, f32[256]{0:T(256)S(1)}, u32[]{:S(2)}, u32[]{:S(2)}) %collective-permute-start.6) | collective-permute-done | bytes 1056 | tf_op jit(solution)/shard_map/ppermute | solution.py:432
  173.5 0.6 add.52
  174.0 0.0 collective-permute-start.3
  174.0 6.6 %shard_map.96.back_ref = f32[1024,8,128]{2,1,0:T(8,128)} custom-call(s32[1]{0:T(128)} %bitcast.mine_ref, bf16[2,512,512]{2,1,0:T(8,128)(2,1)} %bitcast.45, bf16[512,1024]{1,0:T(8,128)(2,1)} %get-tuple-element.24.grad_hidden_ref, bf16[64,16,1024]{2,1,0:T(8,128)(2,1)} %all-to-all-done.other_ref), custom_call_target="tpu_custom_call" | custom-call | flops 1073741824 | bytes 6291456 | tf_op jit(solution)/shard_map/pallas_call | solution.py:367
  180.7 9.7 %all-to-all-done.5.arrived_ref = bf16[64,16,1024]{2,1,0:T(8,128)(2,1)} async-done(((bf16[64,16,1024]{2,1,0:T(8,128)(2,1)}), bf16[64,16,1024]{2,1,0:T(8,128)(2,1)}, u32[]{:S(2)}, u32[]{:S(2)}) %all-to-all-start.5) | async-done | bytes 2097184 | tf_op jit(solution)/shard_map/all_to_all | solution.py:413
  190.4 6.6 %shard_map.97 = f32[1024,2,8,128]{3,2,1,0:T(8,128)} custom-call(s32[1]{0:T(128)} %bitcast.mine_ref, f32[1024,8,128]{2,1,0:T(8,128)} %shard_map.96.back_ref, bf16[64,16,1024]{2,1,0:T(8,128)(2,1)} %all-to-all-done.5.arrived_ref), custom_call_target="tpu_custom_call" | custom-call | bytes 14680064 | tf_op jit(solution)/shard_map/pallas_call | solution.py:388
  197.0 0.0 collective-permute-done.4
  197.0 0.8 pad_maximum_fusion
  197.9 0.0 collective-permute-done.3
  197.9 0.9 bitcast_add_fusion.1
  (8 shorter events, 0.2 us)
Async XLA Ops:
  5.3 63.9 %all-to-all-start = ((bf16[64,16,1024]{2,1,0:T(8,128)(2,1)}), bf16[64,16,1024]{2,1,0:T(8,128)(2,1)}, u32[]{:S(2)}, u32[]{:S(2)}) async-start(bf16[64,16,1024]{2,1,0:T(8,128)(2,1)} %shard_map.93), calls=%async_computation | async-start | bytes 4194304 | tf_op jit(solution)/shard_map/all_to_all | solution.py:413
  22.8 46.4 %copy-start = (bf16[2,512,1024]{2,1,0:T(8,128)(2,1)S(1)}, bf16[2,512,1024]{2,1,0:T(8,128)(2,1)}, u32[]{:S(2)}) copy-start(bf16[2,512,1024]{2,1,0:T(8,128)(2,1)} %shard_map.92.own_ref) | copy-start | bytes 6291460
  72.3 17.1 %copy-start.1 = (bf16[2,512,1024]{2,1,0:T(8,128)(2,1)}, bf16[2,512,1024]{2,1,0:T(8,128)(2,1)S(1)}, u32[]{:S(2)}) copy-start(bf16[2,512,1024]{2,1,0:T(8,128)(2,1)S(1)} %get-tuple-element.20) | copy-start | bytes 6291460
  104.0 16.3 %copy-start.6 = (bf16[512,256]{1,0:T(8,128)(2,1)S(1)}, bf16[512,256]{1,0:T(8,128)(2,1)}, u32[]{:S(2)}) copy-start(bf16[512,256]{1,0:T(8,128)(2,1)} %second_ref.1) | copy-start | bytes 786436
  104.0 17.1 %copy-start.9 = (f32[256]{0:T(256)S(1)}, f32[256]{0:T(256)}, u32[]{:S(2)}) copy-start(f32[256]{0:T(256)} %param.8) | copy-start | bytes 3076
  116.8 14.9 %all-to-all-start.4 = ((bf16[8,64,1024]{2,1,0:T(8,128)(2,1)}), bf16[8,64,1024]{2,1,0:T(8,128)(2,1)S(1)}, u32[]{:S(2)}, u32[]{:S(2)}) async-start(bf16[8,64,1024]{2,1,0:T(8,128)(2,1)} %broadcast_in_dim.15), calls=%async_computation.4 | async-start | bytes 2097152 | tf_op jit(solution)/shard_map/all_to_all | solution.py:413
  131.6 1.0 copy-start.3
  139.0 5.9 %copy-start.2 = (bf16[2,512,1024]{2,1,0:T(8,128)(2,1)S(1)}, bf16[2,512,1024]{2,1,0:T(8,128)(2,1)}, u32[]{:S(2)}) copy-start(bf16[2,512,1024]{2,1,0:T(8,128)(2,1)} %copy-done.1) | copy-start | bytes 6291460
  139.0 5.9 %copy-start.5 = (bf16[512,1024]{1,0:T(8,128)(2,1)S(1)}, bf16[512,1024]{1,0:T(8,128)(2,1)}, u32[]{:S(2)}) copy-start(bf16[512,1024]{1,0:T(8,128)(2,1)} %get-tuple-element.24.grad_hidden_ref) | copy-start | bytes 3145732
  139.0 51.4 %all-to-all-start.5 = ((bf16[64,16,1024]{2,1,0:T(8,128)(2,1)}), bf16[64,16,1024]{2,1,0:T(8,128)(2,1)}, u32[]{:S(2)}, u32[]{:S(2)}) async-start(bf16[64,16,1024]{2,1,0:T(8,128)(2,1)} %get-tuple-element.25), calls=%async_computation.5 | async-start | bytes 4194304 | tf_op jit(solution)/shard_map/all_to_all | solution.py:413
  146.2 1.3 copy-start.4
  147.5 1.0 copy-start.7
  147.6 3.2 %collective-permute-start = (f32[2,2,16,8,512]{4,3,2,1,0:T(8,128)S(1)}, f32[2,2,16,8,512]{4,3,2,1,0:T(8,128)S(1)}, u32[]{:S(2)}, u32[]{:S(2)}) collective-permute-start(f32[2,2,16,8,512]{4,3,2,1,0:T(8,128)S(1)} %dynamic-slice_bitcast_fusion), channel_id=1, source_target_pairs={{0,64},{64,0},{128,192},{192,128},{1,65},{65,1},{129,193},{193,129... | collective-permute-start | bytes 3145736 | tf_op jit(solution)/shard_map/ppermute | solution.py:432
  148.6 2.1 %collective-permute-start.1 = (f32[256,256]{1,0:T(8,128)S(1)}, f32[256,256]{1,0:T(8,128)S(1)}, u32[]{:S(2)}, u32[]{:S(2)}) collective-permute-start(f32[256,256]{1,0:T(8,128)S(1)} %dynamic-slice_bitcast_fusion.1), channel_id=1, source_target_pairs={{0,64},{64,0},{128,192},{192,128},{1,65},{65,1},{129,193},{193,129... | collective-permute-start | bytes 786440 | tf_op jit(solution)/shard_map/ppermute | solution.py:432
  150.8 16.1 %copy-start.8 = (f32[256,1]{1,0:T(8,128)S(1)}, f32[256,1]{1,0:T(8,128)}, u32[]{:S(2)}) copy-start(f32[256,1]{1,0:T(8,128)} %get-tuple-element.30) | copy-start | bytes 3076
  152.3 14.4 %collective-permute-start.2 = (f32[256,256]{1,0:T(8,128)S(1)}, f32[256,256]{1,0:T(8,128)S(1)}, u32[]{:S(2)}, u32[]{:S(2)}) collective-permute-start(f32[256,256]{1,0:T(8,128)S(1)} %bitcast_add_fusion.2), channel_id=1, source_target_pairs={{0,128},{128,0},{64,192},{192,64},{1,129},{129,1},{65,193},{193,65... | collective-permute-start | bytes 786440 | tf_op jit(solution)/shard_map/ppermute | solution.py:432
  166.8 30.3 %collective-permute-start.4 = (f32[256,256]{1,0:T(8,128)S(1)}, f32[256,256]{1,0:T(8,128)S(1)}, u32[]{:S(2)}, u32[]{:S(2)}) collective-permute-start(f32[256,256]{1,0:T(8,128)S(1)} %add.48), channel_id=1, source_target_pairs={{0,64},{64,0},{128,192},{192,128},{1,65},{65,1},{129,193},{193,129... | collective-permute-start | bytes 786440 | tf_op jit(solution)/shard_map/ppermute | solution.py:432
  167.0 1.4 collective-permute-start.5
  168.4 5.1 %collective-permute-start.6 = (f32[256]{0:T(256)S(1)}, f32[256]{0:T(256)S(1)}, u32[]{:S(2)}, u32[]{:S(2)}) collective-permute-start(f32[256]{0:T(256)S(1)} %add.51), channel_id=1, source_target_pairs={{0,128},{128,0},{64,192},{192,64},{1,129},{129,1},{65,193},{193,65... | collective-permute-start | bytes 3080 | tf_op jit(solution)/shard_map/ppermute | solution.py:432
  174.0 23.9 %collective-permute-start.3 = (bf16[2,16,8,512]{3,2,1,0:T(8,128)(2,1)S(1)}, bf16[2,16,8,512]{3,2,1,0:T(8,128)(2,1)S(1)}, u32[]{:S(2)}, u32[]{:S(2)}) collective-permute-start(bf16[2,16,8,512]{3,2,1,0:T(8,128)(2,1)S(1)} %fusion.2), channel_id=1, source_target_pairs={{0,128},{128,0},{64,192},{192,64},{1,129},{129,1},{65,193},{193,65... | collective-permute-start | bytes 786440 | tf_op jit(solution)/shard_map/ppermute | solution.py:432
where the time goes:
time: 199 us
  waiting for transfers between devices  85.6 us (43%)
  blocking collectives  43.2 us (22%)
  Pallas kernels  31.9 us (16%)
  starting transfers between devices  24.1 us (12%)
  local copies, waits for them, and re-layouts  7.67 us (4%)
  other arithmetic  4.14 us (2%)
    all_to_all x3, waiting for transfers between devices, exchange(): lax.all_to_all(blocks, 'field', 0, 0, axis_index_groups=groups, tiled=True)  64.2 us
    all_to_all x3, blocking collectives, exchange(): lax.all_to_all(blocks, 'field', 0, 0, axis_index_groups=groups, tiled=True)  43.2 us
    all_to_all x3, starting transfers between devices, exchange(): lax.all_to_all(blocks, 'field', 0, 0, axis_index_groups=groups, tiled=True)  22.3 us
    ppermute x7, waiting for transfers between devices, swap(): return lax.ppermute(value, 'batch', pairs)  21.4 us
    pallas_call x2, Pallas kernels, turn_call(): pl.pallas_call(kernel, grid=(rows // block,), in_specs=[SMEM_SPEC, pl.Blo...  9.2 us
    pallas_call x1, Pallas kernels, turn_own_grads(): pl.pallas_call(own_back_kernel, grid=(rows // block,), in_specs=[SMEM_SPE...  6.65 us
    pallas_call x1, Pallas kernels, join_grads(): pl.pallas_call(final_kernel, grid=(rows // block,), in_specs=[SMEM_SPEC,...  6.58 us
    pallas_call x1, Pallas kernels, run_head(): pl.pallas_call(head_kernel, grid=(rows // block,), in_specs=[SMEM_SPEC, p...  6.45 us
  transfers between devices with their start and end apart: 10, of which 7 were waited for; matrix products, arithmetic and copies ran while one was open for 4% of the time, Pallas kernels for 9%

commit v1 on v0

--- a/solution.py
+++ b/solution.py
@@ -5,9 +5,10 @@
 from jax.experimental.pallas import tpu as pltpu
 from jax.sharding import PartitionSpec as P
 
-PLANE = 8
+PLANE = 16
 LANES = 128
 TURN = 512
+CHUNKS = 2
 MIB = 1024 * 1024
 CORE_PAIRS = [(0, 1), (1, 0), (2, 3), (3, 2)]
 FAR_PAIRS = [(0, 2), (2, 0), (1, 3), (3, 1)]
@@ -137,26 +138,31 @@
     )
 
 
-def pairs_kernel(mine_ref, own_ref, other_ref, weights_ref, pairs_ref, partial_ref):
-    half = other_ref.shape[0]
-    rows = other_ref.shape[2]
-    latent = own_ref.shape[1] // half
-    total = None
-    others = other_ref[...].astype(jnp.float32).reshape(half, 2, latent, rows)
+def products(mine_ref, own_ref, other_ref, first):
+    slots, wide, rows = other_ref.shape
+    latent = wide // 2
+    others = other_ref[...].astype(jnp.float32).reshape(slots, 2, latent, rows)
+    parts = []
     for i in range(2):
-        own = own_ref[i].astype(jnp.float32).reshape(half, latent, rows)
-        product = own * others[:, i]
+        part = own_ref[i].astype(jnp.float32).reshape(slots, latent, rows) * others[:, i]
         if i == 0:
-            slot = lax.broadcasted_iota(jnp.int32, product.shape, 0)
-            product = jnp.where(slot == mine_ref[0], 0.0, product)
-        product = product.astype(jnp.bfloat16).reshape(half * latent, rows)
-        pairs_ref[i] = product
-        part = jnp.dot(weights_ref[i], product, preferred_element_type=jnp.float32)
-        total = part if total is None else total + part
+            part = jnp.where(own_slot(mine_ref, part.shape, first), 0.0, part)
+        parts.append(part.astype(jnp.bfloat16).reshape(slots * latent, rows))
+    return parts
+
+
+def own_slot(mine_ref, shape, first):
+    return lax.broadcasted_iota(jnp.int32, shape, 0) + first == mine_ref[0]
+
+
+def pairs_kernel(mine_ref, own_ref, other_ref, weights_ref, partial_ref):
+    first, second = products(mine_ref, own_ref, other_ref, 0)
+    total = jnp.dot(weights_ref[0], first, preferred_element_type=jnp.float32)
+    total += jnp.dot(weights_ref[1], second, preferred_element_type=jnp.float32)
     partial_ref[...] = total.astype(jnp.bfloat16)
 
 
-def make_pairs(mine, own, other, weights_turned):
+def make_partial(mine, own, other, weights_turned):
     _, depth, rows = own.shape
     owners, wide, _ = other.shape
     width = weights_turned.shape[1]
@@ -170,17 +176,39 @@
             pl.BlockSpec((owners, wide, block), lambda at: (0, 0, at)),
             pl.BlockSpec((2, width, depth), lambda at: (0, 0, 0)),
         ],
-        out_specs=[
-            pl.BlockSpec((2, depth, block), lambda at: (0, 0, at)),
-            pl.BlockSpec((width, block), lambda at: (0, at)),
-        ],
-        out_shape=[
-            jax.ShapeDtypeStruct((2, depth, rows), jnp.bfloat16),
-            jax.ShapeDtypeStruct((width, rows), jnp.bfloat16),
-        ],
+        out_specs=pl.BlockSpec((width, block), lambda at: (0, at)),
+        out_shape=jax.ShapeDtypeStruct((width, rows), jnp.bfloat16),
         compiler_params=params(24),
         cost_estimate=cost(4 * depth * rows * width, 16 * depth * rows),
     )(mine, own, other, weights_turned)
+
+
+def grad_first_kernel(mine_ref, own_ref, other_ref, grad_hidden_ref, grads_ref):
+    first = pl.program_id(0) * other_ref.shape[0]
+    for i, pairs in enumerate(products(mine_ref, own_ref, other_ref, first)):
+        grads_ref[i] = lax.dot_general(
+            pairs, grad_hidden_ref[...], NT, preferred_element_type=jnp.float32
+        )
+
+
+def make_grad_first(mine, own, other, grad_hidden):
+    _, depth, rows = own.shape
+    owners, wide, _ = other.shape
+    width = grad_hidden.shape[0]
+    return pl.pallas_call(
+        grad_first_kernel,
+        grid=(CHUNKS,),
+        in_specs=[
+            SMEM_SPEC,
+            pl.BlockSpec((2, depth // CHUNKS, rows), lambda at: (0, at, 0)),
+            pl.BlockSpec((owners // CHUNKS, wide, rows), lambda at: (at, 0, 0)),
+            pl.BlockSpec((width, rows), lambda at: (0, 0)),
+        ],
+        out_specs=pl.BlockSpec((2, depth // CHUNKS, width), lambda at: (0, at, 0)),
+        out_shape=jax.ShapeDtypeStruct((2, depth, width), jnp.float32),
+        compiler_params=params(60),
+        cost_estimate=cost(4 * depth * rows * width, 16 * depth * rows),
+    )(mine, own, other, grad_hidden)
 
 
 def head_kernel(
@@ -198,45 +226,38 @@
     grad_hidden_ref,
     returning_ref,
 ):
-    half = returning_ref.shape[0]
-    rows = returning_ref.shape[2]
-    latent = own_ref.shape[1] // half
-    hidden = hidden_ref[...].astype(jnp.float32)
-    sigmoid_hidden = jax.nn.sigmoid(hidden)
-    activated = (hidden * sigmoid_hidden).astype(jnp.bfloat16)
-    second_pre = jnp.dot(second_turned_ref[...], activated, preferred_element_type=jnp.float32)
-    sigmoid_pre = jax.nn.sigmoid(second_pre)
-    second_act = second_pre * sigmoid_pre
-    out_weight = out_weight_ref[...]
-    upstream = upstream_ref[...]
-    logits_ref[...] = jnp.sum(second_act * out_weight, axis=0, keepdims=True)
-    slope = sigmoid_pre * (1.0 + second_pre * (1.0 - sigmoid_pre))
-    grad_pre = (upstream * out_weight * slope).astype(jnp.bfloat16)
-    grad_second = lax.dot_general(activated, grad_pre, NT, preferred_element_type=jnp.float32)
-    grad_out = jnp.sum(second_act * upstream, axis=1, keepdims=True)
+    slots, wide, rows = returning_ref.shape
+    latent = wide // 2
 
     @pl.when(pl.program_id(0) == 0)
     def _():
-        grad_second_ref[...] = grad_second
-        grad_out_ref[...] = grad_out
-
-    @pl.when(pl.program_id(0) != 0)
-    def _():
-        grad_second_ref[...] += grad_second
-        grad_out_ref[...] += grad_out
-
-    back_hidden = jnp.dot(second_ref[...], grad_pre, preferred_element_type=jnp.float32)
-    slope = sigmoid_hidden * (1.0 + hidden * (1.0 - sigmoid_hidden))
-    grad_hidden = (back_hidden * slope).astype(jnp.bfloat16)
-    grad_hidden_ref[...] = grad_hidden
+        hidden = hidden_ref[...].astype(jnp.float32)
+        sigmoid_hidden = jax.nn.sigmoid(hidden)
+        activated = (hidden * sigmoid_hidden).astype(jnp.bfloat16)
+        second_pre = jnp.dot(second_turned_ref[...], activated, preferred_element_type=jnp.float32)
+        sigmoid_pre = jax.nn.sigmoid(second_pre)
+        second_act = second_pre * sigmoid_pre
+        out_weight = out_weight_ref[...]
+        upstream = upstream_ref[...]
+        logits_ref[...] = jnp.sum(second_act * out_weight, axis=0, keepdims=True)
+        slope = sigmoid_pre * (1.0 + second_pre * (1.0 - sigmoid_pre))
+        grad_pre = (upstream * out_weight * slope).astype(jnp.bfloat16)
+        grad_second_ref[...] = lax.dot_general(
+            activated, grad_pre, NT, preferred_element_type=jnp.float32
+        )
+        grad_out_ref[...] = jnp.sum(second_act * upstream, axis=1, keepdims=True)
+        back_hidden = jnp.dot(second_ref[...], grad_pre, preferred_element_type=jnp.float32)
+        slope = sigmoid_hidden * (1.0 + hidden * (1.0 - sigmoid_hidden))
+        grad_hidden_ref[...] = (back_hidden * slope).astype(jnp.bfloat16)
+
+    first = pl.program_id(0) * slots
     returning = []
     for i in range(2):
-        grads = jnp.dot(weights_ref[i], grad_hidden, preferred_element_type=jnp.float32)
-        grads = grads.reshape(half, latent, rows)
+        grads = jnp.dot(weights_ref[i], grad_hidden_ref[...], preferred_element_type=jnp.float32)
+        grads = grads.reshape(slots, latent, rows)
         if i == 0:
-            slot = lax.broadcasted_iota(jnp.int32, grads.shape, 0)
-            grads = jnp.where(slot == mine_ref[0], 0.0, grads)
-        own = own_ref[i].astype(jnp.float32).reshape(half, latent, rows)
+            grads = jnp.where(own_slot(mine_ref, grads.shape, first), 0.0, grads)
+        own = own_ref[i].astype(jnp.float32).reshape(slots, latent, rows)
         returning.append(grads * own)
     returning = jnp.stack(returning, axis=1).reshape(returning_ref.shape)
     returning_ref[...] = returning.astype(jnp.bfloat16)
@@ -247,28 +268,26 @@
     _, depth, _ = own.shape
     owners, wide = depth // latent, 2 * latent
     width_two = second.shape[1]
-    block = min(rows, 1024)
-    moved = lambda at: (0, 0, at)
     fixed = lambda at: (0, 0)
     return pl.pallas_call(
         head_kernel,
-        grid=(rows // block,),
+        grid=(CHUNKS,),
         in_specs=[
             SMEM_SPEC,
-            pl.BlockSpec((width, block), lambda at: (0, at)),
+            pl.BlockSpec((width, rows), fixed),
             pl.BlockSpec((width, width_two), fixed),
             pl.BlockSpec((width_two, width), fixed),
             pl.BlockSpec((width_two, 1), fixed),
-            pl.BlockSpec((1, block), lambda at: (0, at)),
-            pl.BlockSpec((2, depth, width), lambda at: (0, 0, 0)),
-            pl.BlockSpec((2, depth, block), moved),
+            pl.BlockSpec((1, rows), fixed),
+            pl.BlockSpec((2, depth // CHUNKS, width), lambda at: (0, at, 0)),
+            pl.BlockSpec((2, depth // CHUNKS, rows), lambda at: (0, at, 0)),
         ],
         out_specs=[
-            pl.BlockSpec((1, block), lambda at: (0, at)),
+            pl.BlockSpec((1, rows), fixed),
             pl.BlockSpec((width, width_two), fixed),
             pl.BlockSpec((width_two, 1), fixed),
-            pl.BlockSpec((width, block), lambda at: (0, at)),
-            pl.BlockSpec((owners, wide, block), moved),
+            pl.BlockSpec((width, rows), fixed),
+            pl.BlockSpec((owners // CHUNKS, wide, rows), lambda at: (at, 0, 0)),
         ],
         out_shape=[
             jax.ShapeDtypeStruct((1, rows), jnp.float32),
@@ -396,7 +415,7 @@
         out_specs=pl.BlockSpec((block, 2, latent, lanes), lambda at: (at, 0, 0, 0)),
         out_shape=jax.ShapeDtypeStruct((rows, 2, latent, lanes), jnp.float32),
         scratch_shapes=turn_scratch(block, latent, lanes),
-        compiler_params=params(60),
+        compiler_params=params(48),
         cost_estimate=cost(0, back.size * 14),
     )(mine, back, arrived)
 
@@ -419,12 +438,10 @@
     depth = owners // PLANE
     units, rows = partial.shape
     share = exchange(partial.reshape(PLANE, units // PLANE, rows), inner)
-    share = jnp.sum(share.astype(jnp.float32), axis=0)
-    share = exchange(share.reshape(depth, units // owners, rows), outer)
-    share = jnp.sum(share, axis=0).astype(jnp.bfloat16)
+    share = jnp.sum(share.astype(jnp.float32), axis=0).astype(jnp.bfloat16)
     copies = jnp.broadcast_to(share[None], (depth,) + share.shape)
-    plane = exchange(copies, outer).reshape(units // PLANE, rows)
-    copies = jnp.broadcast_to(plane[None], (PLANE,) + plane.shape)
+    share = jnp.sum(exchange(copies, outer).astype(jnp.float32), axis=0).astype(jnp.bfloat16)
+    copies = jnp.broadcast_to(share[None], (PLANE,) + share.shape)
     return exchange(copies, inner).reshape(units, rows)
 
 
@@ -447,7 +464,7 @@
     weights = first_weight.reshape(local_fields, half * latent, width)
     other = exchange(make_send(mine, turned))
     own = make_own(mine, turned)
-    pairs, partial = make_pairs(mine, own, other, jnp.transpose(weights, (0, 2, 1)))
+    partial = make_partial(mine, own, other, jnp.transpose(weights, (0, 2, 1)))
     hidden = field_sum(partial)
     logits, grad_second, grad_out, grad_hidden, returning = run_head(
         mine, hidden, second_weight, out_weight, upstream, weights, own, latent
@@ -455,9 +472,8 @@
     arrived = exchange(returning)
     place = lax.axis_index("batch")
     far, core = place // 2, place % 2
-    share_first = lax.dot_general(
-        pairs.reshape(-1, pairs.shape[2]), grad_hidden, NT, preferred_element_type=jnp.float32
-    ).reshape(local_fields, 2, 2, half // 4, latent, width)
+    share_first = make_grad_first(mine, own, other, grad_hidden)
+    share_first = share_first.reshape(local_fields, 2, 2, half // 4, latent, width)
     share_first = core_share(share_first, core, 2)
     give_first = part_of(share_first, 1 - far, 1).astype(jnp.bfloat16)
     rows_second, width_second = grad_second.shape
@@ -466,16 +482,18 @@
         (give_first, share_second, grad_hidden)
     )
     take_first = swap(give_first, FAR_PAIRS)
-    share_second = share_second + swap(share_second, FAR_PAIRS)
-    mate_second = swap(share_second, CORE_PAIRS)
+    take_second = swap(share_second, FAR_PAIRS)
     grad_out = grad_out.reshape(-1)
     grad_out = grad_out + swap(grad_out, CORE_PAIRS)
-    grad_out = grad_out + swap(grad_out, FAR_PAIRS)
+    take_out = swap(grad_out, FAR_PAIRS)
     back = turn_own_grads(mine, weights, grad_hidden, other)
+    share_first, share_second, grad_out, back = lax.optimization_barrier(
+        (share_first, share_second, grad_out, back)
+    )
+    grad_out = grad_out + take_out
+    share_second = share_second + take_second
+    mate_second = swap(share_second, CORE_PAIRS)
     grad_vectors = join_grads(mine, back, arrived)
-    share_first, share_second, grad_vectors = lax.optimization_barrier(
-        (share_first, share_second, grad_vectors)
-    )
     grad_first = part_of(share_first, far, 1) + take_first.astype(jnp.float32)
     grad_second = jnp.stack(
         [

time: 199 us -> 192 us (0.965)
  blocking collectives: 43.2 us -> 31.7 us
  waiting for transfers between devices: 85.6 us -> 76.6 us
  other arithmetic: 4.14 us -> 8.72 us
  starting transfers between devices: 24.1 us -> 27.9 us
  Pallas kernels: 31.9 us -> 35.4 us
  local copies, waits for them, and re-layouts: 7.67 us -> 10.1 us
    all_to_all x3 -> x2, blocking collectives: 43.2 us -> 31.7 us  [exchange(): lax.all_to_all(blocks, 'field', 0, 0, axis_index_groups=groups, tiled=True)]
    ppermute x7, waiting for transfers between devices: 21.4 us -> 13.6 us  [swap(): return lax.ppermute(value, 'batch', pairs)]
    ppermute x7, starting transfers between devices: 1.76 us -> 5.56 us  [swap(): return lax.ppermute(value, 'batch', pairs)]
    pallas_call x2 -> x3, Pallas kernels: 9.5 us -> 13.2 us  [the longest x1 5.97 us: run_head(): pl.pallas_call(head_kernel, grid=(CHUNKS,), in_specs=[SMEM_SPEC, pl.Block...]
    dynamic_slice x0 -> x2, local copies, waits for them, and re-layouts: none -> 2.8 us  [part_of(): return lax.dynamic_index_in_dim(value, index, axis, keepdims=False)]
    unnamed x21 -> x17, local copies, waits for them, and re-layouts: 4.02 us -> 2.95 us
  transfers between devices with their start and end apart: 10 -> 10, of which waited for: 7 -> 7; matrix products, arithmetic and copies ran while one was open for 4% -> 8% of each run, Pallas kernels for 9% -> 8%
where the time goes in v1:
time: 192 us; the launch traced here: 191 us
  waiting for transfers between devices  76.6 us (40%)
  Pallas kernels  35.4 us (18%)
  blocking collectives  31.7 us (17%)
  starting transfers between devices  27.9 us (15%)
  local copies, waits for them, and re-layouts  10.1 us (5%)
  other arithmetic  8.72 us (5%)
    all_to_all x3, waiting for transfers between devices, exchange(): lax.all_to_all(blocks, 'field', 0, 0, axis_index_groups=groups, tiled=True)  62.9 us
    all_to_all x2, blocking collectives, exchange(): lax.all_to_all(blocks, 'field', 0, 0, axis_index_groups=groups, tiled=True)  31.7 us
    all_to_all x3, starting transfers between devices, exchange(): lax.all_to_all(blocks, 'field', 0, 0, axis_index_groups=groups, tiled=True)  22.3 us
    ppermute x7, waiting for transfers between devices, swap(): return lax.ppermute(value, 'batch', pairs)  13.6 us
    pallas_call x2, Pallas kernels, turn_call(): pl.pallas_call(kernel, grid=(rows // block,), in_specs=[SMEM_SPEC, pl.Blo...  9.19 us
    pallas_call x1, Pallas kernels, turn_own_grads(): pl.pallas_call(own_back_kernel, grid=(rows // block,), in_specs=[SMEM_SPE...  6.72 us
    pallas_call x1, Pallas kernels, join_grads(): pl.pallas_call(final_kernel, grid=(rows // block,), in_specs=[SMEM_SPEC,...  6.31 us
    pallas_call x1, Pallas kernels, run_head(): pl.pallas_call(head_kernel, grid=(CHUNKS,), in_specs=[SMEM_SPEC, pl.Block...  5.97 us
  transfers between devices with their start and end apart: 10, of which 7 were waited for; matrix products, arithmetic and copies ran while one was open for 8% of the time, Pallas kernels for 8%

profile of v1, /device:TPU:16, one launch (start us, length us, event | category | flops | bytes accessed | tf_op | source)
XLA Modules:
  0.0 191.2 jit_solution(9927283445053408223)
XLA Ops:
  0.6 4.6 %shard_map.93 = bf16[64,16,1024]{2,1,0:T(8,128)(2,1)} custom-call(s32[1]{0:T(128)} %bitcast.mine_ref, bf16[1024,2,8,128]{3,2,1,0:T(8,128)(2,1)} %bitcast.33), custom_call_target="tpu_custom_call" | custom-call | bytes 6291456 | tf_op jit(solution)/shard_map/pallas_call | solution.py:98
  5.3 12.9 %all-to-all-start = ((bf16[64,16,1024]{2,1,0:T(8,128)(2,1)}), bf16[64,16,1024]{2,1,0:T(8,128)(2,1)}, u32[]{:S(2)}, u32[]{:S(2)}) async-start(bf16[64,16,1024]{2,1,0:T(8,128)(2,1)} %shard_map.93), calls=%async_computation | async-start | bytes 4194304 | tf_op jit(solution)/shard_map/all_to_all | solution.py:432
  18.2 4.6 %shard_map.92.own_ref = bf16[2,512,1024]{2,1,0:T(8,128)(2,1)} custom-call(s32[1]{0:T(128)} %bitcast.mine_ref, bf16[1024,2,8,128]{3,2,1,0:T(8,128)(2,1)} %bitcast.34), custom_call_target="tpu_custom_call" | custom-call | bytes 6291456 | tf_op jit(solution)/shard_map/pallas_call | solution.py:98
  22.7 0.0 copy-start
  22.8 1.6 copy.19.weights_ref
  24.4 44.8 %all-to-all-done.other_ref = bf16[64,16,1024]{2,1,0:T(8,128)(2,1)} async-done(((bf16[64,16,1024]{2,1,0:T(8,128)(2,1)}), bf16[64,16,1024]{2,1,0:T(8,128)(2,1)}, u32[]{:S(2)}, u32[]{:S(2)}) %all-to-all-start) | async-done | bytes 2097184 | tf_op jit(solution)/shard_map/all_to_all | solution.py:432
  69.2 0.0 copy-done
  69.2 2.8 %shard_map.94 = bf16[512,1024]{1,0:T(8,128)(2,1)S(1)} custom-call(s32[1]{0:T(128)} %bitcast.mine_ref, bf16[2,512,1024]{2,1,0:T(8,128)(2,1)S(1)} %copy-done, bf16[64,16,1024]{2,1,0:T(8,128)(2,1)} %all-to-all-done.other_ref, bf16[2,512,512]{2,1,0:T(8,128)(2,1)S(1)} %copy.19.weights_ref), custom_call_target="tpu_custom_call" | custom-call | flops 1073741824 | bytes 8388608 | tf_op jit(solution)/shard_map/pallas_call | solution.py:170
  72.1 19.1 %all_to_all.25 = bf16[16,32,1024]{2,1,0:T(8,128)(2,1)S(1)} all-to-all(bf16[16,32,1024]{2,1,0:T(8,128)(2,1)S(1)} %bitcast.32), channel_id=1, replica_groups={{0,1,2,3,4,5,6,7,8,9,10,11,12,13,14,15},{16,17,18,19,20,21,22,23,24,25,..., dimensions={0} | all-to-all | bytes 2097152 | tf_op jit(solution)/shard_map/all_to_all | solution.py:432
  91.2 0.2 reduce_sum.24
  91.4 0.0 copy-start.7
  91.4 0.0 copy-start.4
  91.4 12.6 %all_to_all.26 = bf16[4,32,1024]{2,1,0:T(8,128)(2,1)S(1)} all-to-all(bf16[4,32,1024]{2,1,0:T(8,128)(2,1)S(1)} %broadcast_in_dim.4), channel_id=1, replica_groups={{0,16,32,48},{1,17,33,49},{2,18,34,50},{3,19,35,51},{4,20,36,52},{5,21,..., dimensions={0} | all-to-all | bytes 524288 | tf_op jit(solution)/shard_map/all_to_all | solution.py:432
  104.1 1.1 broadcast_in_dim.5
  105.2 3.7 %all-to-all-start.3 = ((bf16[16,32,1024]{2,1,0:T(8,128)(2,1)}), bf16[16,32,1024]{2,1,0:T(8,128)(2,1)S(1)}, u32[]{:S(2)}, u32[]{:S(2)}) async-start(bf16[16,32,1024]{2,1,0:T(8,128)(2,1)} %broadcast_in_dim.5), calls=%async_computation.3 | async-start | bytes 2097152 | tf_op jit(solution)/shard_map/all_to_all | solution.py:432
  108.9 0.0 copy-done.7
  108.9 0.8 copy.21.out_weight_ref
  109.7 0.0 copy-done.4
  109.7 0.8 copy.20
  110.6 12.4 %all-to-all-done.3 = bf16[16,32,1024]{2,1,0:T(8,128)(2,1)S(1)} async-done(((bf16[16,32,1024]{2,1,0:T(8,128)(2,1)}), bf16[16,32,1024]{2,1,0:T(8,128)(2,1)S(1)}, u32[]{:S(2)}, u32[]{:S(2)}) %all-to-all-start.3) | async-done | bytes 1048608 | tf_op jit(solution)/shard_map/all_to_all | solution.py:432
  123.0 0.0 copy-start.1
  123.0 1.0 copy-done.1
  123.9 6.0 %shard_map.95 = (f32[1,1024]{1,0:T(1,128)}, f32[512,256]{1,0:T(8,128)}, f32[256,1]{1,0:T(8,128)}, bf16[512,1024]{1,0:T(8,128)(2,1)}, bf16[64,16,1024]{2,1,0:T(8,128)(2,1)}) custom-call(s32[1]{0:T(128)} %bitcast.mine_ref, bf16[512,1024]{1,0:T(8,128)(2,1)} %bitcast.40, bf16[512,256]{1,0:T(8,128)(2,1)} %second_ref.1, bf16[256,512]{1,0:T(8,128)(2,1)} %bitcast.41, ...), custom_call_target="tpu_custom_call" | custom-call | flops 1073741824 | bytes 12582912 | tf_op jit(solution)/shard_map/pallas_call | solution.py:272
  129.9 5.7 %all-to-all-start.4 = ((bf16[64,16,1024]{2,1,0:T(8,128)(2,1)}), bf16[64,16,1024]{2,1,0:T(8,128)(2,1)S(1)}, u32[]{:S(2)}, u32[]{:S(2)}) async-start(bf16[64,16,1024]{2,1,0:T(8,128)(2,1)} %get-tuple-element.24), calls=%async_computation.4 | async-start | bytes 4194304 | tf_op jit(solution)/shard_map/all_to_all | solution.py:432
  135.6 4.4 %shard_map.96 = f32[2,512,512]{2,1,0:T(8,128)} custom-call(s32[1]{0:T(128)} %bitcast.mine_ref, bf16[2,512,1024]{2,1,0:T(8,128)(2,1)} %shard_map.92.own_ref, bf16[64,16,1024]{2,1,0:T(8,128)(2,1)} %all-to-all-done.other_ref, bf16[512,1024]{1,0:T(8,128)(2,1)} %get-tuple-element.22.grad_hidden_ref), custom_call_target="tpu_custom_call" | custom-call | flops 1073741824 | bytes 8388608 | tf_op jit(solution)/shard_map/pallas_call | solution.py:198
  140.0 1.8 constant_dynamic-slice_fusion.1
  141.8 0.0 copy-start.5
  141.8 1.0 copy.26
  142.8 0.0 collective-permute-start
  142.8 0.1 copy-done.5
  143.0 0.5 collective-permute-start.1
  143.4 0.0 copy-start.6
  143.4 2.5 %collective-permute-done.1 = f32[256,256]{1,0:T(8,128)} collective-permute-done((f32[256,256]{1,0:T(8,128)S(1)}, f32[256,256]{1,0:T(8,128)}, u32[]{:S(2)}, u32[]{:S(2)}) %collective-permute-start.1) | collective-permute-done | bytes 262176 | tf_op jit(solution)/shard_map/ppermute | solution.py:449
  146.0 1.1 bitcast_add_fusion.2
  147.0 0.0 collective-permute-done
  147.0 1.4 bitcast_add_fusion
  148.5 0.0 copy-start.2
  148.5 1.0 copy-done.2
  149.5 0.7 fusion
  150.2 0.6 collective-permute-start.4
  150.8 2.9 %collective-permute-start.3 = (bf16[2,16,8,512]{3,2,1,0:T(8,128)(2,1)}, bf16[2,16,8,512]{3,2,1,0:T(8,128)(2,1)}, u32[]{:S(2)}, u32[]{:S(2)}) collective-permute-start(bf16[2,16,8,512]{3,2,1,0:T(8,128)(2,1)} %fusion), channel_id=1, source_target_pairs={{0,128},{128,0},{64,192},{192,64},{1,129},{129,1},{65,193},{193,65... | collective-permute-start | bytes 786440 | tf_op jit(solution)/shard_map/ppermute | solution.py:449
  153.7 0.0 copy-done.6
  153.7 0.1 reduce.2
  153.8 0.3 collective-permute-start.2
  154.1 1.1 collective-permute-done.2
  155.2 0.0 copy-start.3
  155.2 6.7 %shard_map.97.back_ref = f32[1024,8,128]{2,1,0:T(8,128)} custom-call(s32[1]{0:T(128)} %bitcast.mine_ref, bf16[2,512,512]{2,1,0:T(8,128)(2,1)} %bitcast.37, bf16[512,1024]{1,0:T(8,128)(2,1)} %get-tuple-element.22.grad_hidden_ref, bf16[64,16,1024]{2,1,0:T(8,128)(2,1)} %all-to-all-done.other_ref), custom_call_target="tpu_custom_call" | custom-call | flops 1073741824 | bytes 6291456 | tf_op jit(solution)/shard_map/pallas_call | solution.py:386
  162.0 3.5 %collective-permute-done.4 = f32[256,256]{1,0:T(8,128)} collective-permute-done((f32[256,256]{1,0:T(8,128)S(1)}, f32[256,256]{1,0:T(8,128)}, u32[]{:S(2)}, u32[]{:S(2)}) %collective-permute-start.4) | collective-permute-done | bytes 262176 | tf_op jit(solution)/shard_map/ppermute | solution.py:449
  165.5 1.7 add.51
  167.1 0.0 collective-permute-start.5
  167.1 1.3 collective-permute-start.6
  168.4 6.5 %collective-permute-done.6 = f32[256]{0:T(256)S(1)} collective-permute-done((f32[256]{0:T(256)S(1)}, f32[256]{0:T(256)S(1)}, u32[]{:S(2)}, u32[]{:S(2)}) %collective-permute-start.6) | collective-permute-done | bytes 1056 | tf_op jit(solution)/shard_map/ppermute | solution.py:449
  174.9 0.6 add.52
  175.5 0.0 collective-permute-done.3
  175.5 0.0 copy-done.3
  175.5 1.8 bitcast_add_fusion.1
  177.3 0.0 collective-permute-done.5
  177.3 1.0 select_bitcast_fusion.1
  178.3 0.8 pad_maximum_fusion
  179.1 5.8 %all-to-all-done.4.arrived_ref = bf16[64,16,1024]{2,1,0:T(8,128)(2,1)S(1)} async-done(((bf16[64,16,1024]{2,1,0:T(8,128)(2,1)}), bf16[64,16,1024]{2,1,0:T(8,128)(2,1)S(1)}, u32[]{:S(2)}, u32[]{:S(2)}) %all-to-all-start.4) | async-done | bytes 2097184 | tf_op jit(solution)/shard_map/all_to_all | solution.py:432
  184.9 6.3 %shard_map.98 = f32[1024,2,8,128]{3,2,1,0:T(8,128)} custom-call(s32[1]{0:T(128)} %bitcast.mine_ref, f32[1024,8,128]{2,1,0:T(8,128)} %shard_map.97.back_ref, bf16[64,16,1024]{2,1,0:T(8,128)(2,1)S(1)} %all-to-all-done.4.arrived_ref), custom_call_target="tpu_custom_call" | custom-call | bytes 14680064 | tf_op jit(solution)/shard_map/pallas_call | solution.py:407
  (4 shorter events, 0.1 us)
Async XLA Ops:
  5.3 63.9 %all-to-all-start = ((bf16[64,16,1024]{2,1,0:T(8,128)(2,1)}), bf16[64,16,1024]{2,1,0:T(8,128)(2,1)}, u32[]{:S(2)}, u32[]{:S(2)}) async-start(bf16[64,16,1024]{2,1,0:T(8,128)(2,1)} %shard_map.93), calls=%async_computation | async-start | bytes 4194304 | tf_op jit(solution)/shard_map/all_to_all | solution.py:432
  22.7 46.4 %copy-start = (bf16[2,512,1024]{2,1,0:T(8,128)(2,1)S(1)}, bf16[2,512,1024]{2,1,0:T(8,128)(2,1)}, u32[]{:S(2)}) copy-start(bf16[2,512,1024]{2,1,0:T(8,128)(2,1)} %shard_map.92.own_ref) | copy-start | bytes 6291460
  91.4 17.5 %copy-start.7 = (f32[256]{0:T(256)S(1)}, f32[256]{0:T(256)}, u32[]{:S(2)}) copy-start(f32[256]{0:T(256)} %param.8) | copy-start | bytes 3076
  91.4 18.3 %copy-start.4 = (bf16[512,256]{1,0:T(8,128)(2,1)S(1)}, bf16[512,256]{1,0:T(8,128)(2,1)}, u32[]{:S(2)}) copy-start(bf16[512,256]{1,0:T(8,128)(2,1)} %second_ref.1) | copy-start | bytes 786436
  105.2 17.8 %all-to-all-start.3 = ((bf16[16,32,1024]{2,1,0:T(8,128)(2,1)}), bf16[16,32,1024]{2,1,0:T(8,128)(2,1)S(1)}, u32[]{:S(2)}, u32[]{:S(2)}) async-start(bf16[16,32,1024]{2,1,0:T(8,128)(2,1)} %broadcast_in_dim.5), calls=%async_computation.3 | async-start | bytes 2097152 | tf_op jit(solution)/shard_map/all_to_all | solution.py:432
  123.0 1.0 copy-start.1
  129.9 55.0 %all-to-all-start.4 = ((bf16[64,16,1024]{2,1,0:T(8,128)(2,1)}), bf16[64,16,1024]{2,1,0:T(8,128)(2,1)S(1)}, u32[]{:S(2)}, u32[]{:S(2)}) async-start(bf16[64,16,1024]{2,1,0:T(8,128)(2,1)} %get-tuple-element.24), calls=%async_computation.4 | async-start | bytes 4194304 | tf_op jit(solution)/shard_map/all_to_all | solution.py:432
  141.8 1.2 copy-start.5
  142.8 4.2 %collective-permute-start = (f32[2,2,16,8,512]{4,3,2,0,1:T(8,128)}, f32[2,2,16,8,512]{4,3,2,0,1:T(8,128)}, u32[]{:S(2)}, u32[]{:S(2)}) collective-permute-start(f32[2,2,16,8,512]{4,3,2,0,1:T(8,128)} %bitcast.31), channel_id=1, source_target_pairs={{0,64},{64,0},{128,192},{192,128},{1,65},{65,1},{129,193},{193,129... | collective-permute-start | bytes 3145736 | tf_op jit(solution)/shard_map/ppermute | solution.py:449
  143.0 3.0 %collective-permute-start.1 = (f32[256,256]{1,0:T(8,128)S(1)}, f32[256,256]{1,0:T(8,128)}, u32[]{:S(2)}, u32[]{:S(2)}) collective-permute-start(f32[256,256]{1,0:T(8,128)S(1)} %dynamic-slice_bitcast_fusion), channel_id=1, source_target_pairs={{0,64},{64,0},{128,192},{192,128},{1,65},{65,1},{129,193},{193,129... | collective-permute-start | bytes 786440 | tf_op jit(solution)/shard_map/ppermute | solution.py:449
  143.4 10.3 %copy-start.6 = (f32[256,1]{1,0:T(8,128)S(1)}, f32[256,1]{1,0:T(8,128)}, u32[]{:S(2)}) copy-start(f32[256,1]{1,0:T(8,128)} %get-tuple-element.21) | copy-start | bytes 3076
  148.5 1.0 copy-start.2
  150.2 15.3 %collective-permute-start.4 = (f32[256,256]{1,0:T(8,128)S(1)}, f32[256,256]{1,0:T(8,128)}, u32[]{:S(2)}, u32[]{:S(2)}) collective-permute-start(f32[256,256]{1,0:T(8,128)S(1)} %bitcast_add_fusion.2), channel_id=1, source_target_pairs={{0,128},{128,0},{64,192},{192,64},{1,129},{129,1},{65,193},{193,65... | collective-permute-start | bytes 786440 | tf_op jit(solution)/shard_map/ppermute | solution.py:449
  150.8 24.6 %collective-permute-start.3 = (bf16[2,16,8,512]{3,2,1,0:T(8,128)(2,1)}, bf16[2,16,8,512]{3,2,1,0:T(8,128)(2,1)}, u32[]{:S(2)}, u32[]{:S(2)}) collective-permute-start(bf16[2,16,8,512]{3,2,1,0:T(8,128)(2,1)} %fusion), channel_id=1, source_target_pairs={{0,128},{128,0},{64,192},{192,64},{1,129},{129,1},{65,193},{193,65... | collective-permute-start | bytes 786440 | tf_op jit(solution)/shard_map/ppermute | solution.py:449
  153.8 1.4 collective-permute-start.2
  155.2 20.2 %copy-start.3 = (f32[2,2,16,8,512]{4,3,2,0,1:T(8,128)S(1)}, f32[2,2,16,8,512]{4,3,2,0,1:T(8,128)}, u32[]{:S(2)}) copy-start(f32[2,2,16,8,512]{4,3,2,0,1:T(8,128)} %copy-done.2) | copy-start | bytes 3145732
  167.1 10.1 %collective-permute-start.5 = (f32[256,256]{1,0:T(8,128)}, f32[256,256]{1,0:T(8,128)S(1)}, u32[]{:S(2)}, u32[]{:S(2)}) collective-permute-start(f32[256,256]{1,0:T(8,128)} %add.51), channel_id=1, source_target_pairs={{0,64},{64,0},{128,192},{192,128},{1,65},{65,1},{129,193},{193,129... | collective-permute-start | bytes 786440 | tf_op jit(solution)/shard_map/ppermute | solution.py:449
  167.1 7.7 %collective-permute-start.6 = (f32[256]{0:T(256)S(1)}, f32[256]{0:T(256)S(1)}, u32[]{:S(2)}, u32[]{:S(2)}) collective-permute-start(f32[256]{0:T(256)S(1)} %add.48), channel_id=1, source_target_pairs={{0,128},{128,0},{64,192},{192,64},{1,129},{129,1},{65,193},{193,65... | collective-permute-start | bytes 3080 | tf_op jit(solution)/shard_map/ppermute | solution.py:449

commit v2 on v1

--- a/solution.py
+++ b/solution.py
@@ -237,7 +237,7 @@
         second_pre = jnp.dot(second_turned_ref[...], activated, preferred_element_type=jnp.float32)
         sigmoid_pre = jax.nn.sigmoid(second_pre)
         second_act = second_pre * sigmoid_pre
-        out_weight = out_weight_ref[...]
+        out_weight = out_weight_ref[:, :1]
         upstream = upstream_ref[...]
         logits_ref[...] = jnp.sum(second_act * out_weight, axis=0, keepdims=True)
         slope = sigmoid_pre * (1.0 + second_pre * (1.0 - sigmoid_pre))
@@ -263,7 +263,9 @@
     returning_ref[...] = returning.astype(jnp.bfloat16)
 
 
-def run_head(mine, hidden, second, out_weight, upstream, weights, own, latent):
+def run_head(
+    mine, hidden, second, second_turned, out_columns, upstream, weights, own, latent
+):
     width, rows = hidden.shape
     _, depth, _ = own.shape
     owners, wide = depth // latent, 2 * latent
@@ -277,7 +279,7 @@
             pl.BlockSpec((width, rows), fixed),
             pl.BlockSpec((width, width_two), fixed),
             pl.BlockSpec((width_two, width), fixed),
-            pl.BlockSpec((width_two, 1), fixed),
+            pl.BlockSpec((width_two, LANES), fixed),
             pl.BlockSpec((1, rows), fixed),
             pl.BlockSpec((2, depth // CHUNKS, width), lambda at: (0, at, 0)),
             pl.BlockSpec((2, depth // CHUNKS, rows), lambda at: (0, at, 0)),
@@ -302,8 +304,8 @@
         mine,
         hidden,
         second,
-        second.T,
-        out_weight.reshape(width_two, 1),
+        second_turned,
+        out_columns,
         upstream.reshape(1, rows),
         weights,
         own,
@@ -463,11 +465,22 @@
     turned = jnp.transpose(vectors, (0, 1, 3, 2))
     weights = first_weight.reshape(local_fields, half * latent, width)
     other = exchange(make_send(mine, turned))
-    own = make_own(mine, turned)
+    out_columns = jnp.broadcast_to(out_weight[:, None], (out_weight.shape[0], LANES))
+    own, second_turned, out_columns = lax.optimization_barrier(
+        (make_own(mine, turned), second_weight.T, out_columns)
+    )
     partial = make_partial(mine, own, other, jnp.transpose(weights, (0, 2, 1)))
     hidden = field_sum(partial)
     logits, grad_second, grad_out, grad_hidden, returning = run_head(
-        mine, hidden, second_weight, out_weight, upstream, weights, own, latent
+        mine,
+        hidden,
+        second_weight,
+        second_turned,
+        out_columns,
+        upstream,
+        weights,
+        own,
+        latent,
     )
     arrived = exchange(returning)
     place = lax.axis_index("batch")

time: 192 us -> 186 us (0.969)
  blocking collectives: 31.7 us -> 48.1 us
  waiting for transfers between devices: 76.6 us -> 61.4 us
  starting transfers between devices: 27.9 us -> 22.9 us
  local copies, waits for them, and re-layouts: 10.1 us -> 7.89 us
    all_to_all x3 -> x2, waiting for transfers between devices: 62.9 us -> 45.5 us  [exchange(): lax.all_to_all(blocks, 'field', 0, 0, axis_index_groups=groups, tiled=True)]
    all_to_all x2 -> x3, blocking collectives: 31.7 us -> 48.1 us  [exchange(): lax.all_to_all(blocks, 'field', 0, 0, axis_index_groups=groups, tiled=True)]
    all_to_all x3 -> x2, starting transfers between devices: 22.3 us -> 18.7 us  [exchange(): lax.all_to_all(blocks, 'field', 0, 0, axis_index_groups=groups, tiled=True)]
    ppermute x7, waiting for transfers between devices: 13.6 us -> 15.9 us  [swap(): return lax.ppermute(value, 'batch', pairs)]
  transfers between devices with their start and end apart: 10 -> 9, of which waited for: 7 -> 6; matrix products, arithmetic and copies ran while one was open for 8% -> 8% of each run, Pallas kernels for 8% -> 8%
where the time goes in v2:
time: 186 us; the launch traced here: 185 us
  waiting for transfers between devices  61.4 us (33%)
  blocking collectives  48.1 us (26%)
  Pallas kernels  35.5 us (19%)
  starting transfers between devices  22.9 us (12%)
  other arithmetic  8.75 us (5%)
  local copies, waits for them, and re-layouts  7.89 us (4%)
    all_to_all x3, blocking collectives, exchange(): lax.all_to_all(blocks, 'field', 0, 0, axis_index_groups=groups, tiled=True)  48.1 us
    all_to_all x2, waiting for transfers between devices, exchange(): lax.all_to_all(blocks, 'field', 0, 0, axis_index_groups=groups, tiled=True)  45.5 us
    all_to_all x2, starting transfers between devices, exchange(): lax.all_to_all(blocks, 'field', 0, 0, axis_index_groups=groups, tiled=True)  18.7 us
    ppermute x7, waiting for transfers between devices, swap(): return lax.ppermute(value, 'batch', pairs)  15.9 us
    pallas_call x2, Pallas kernels, turn_call(): pl.pallas_call(kernel, grid=(rows // block,), in_specs=[SMEM_SPEC, pl.Blo...  9.21 us
    pallas_call x1, Pallas kernels, turn_own_grads(): pl.pallas_call(own_back_kernel, grid=(rows // block,), in_specs=[SMEM_SPE...  6.72 us
    pallas_call x1, Pallas kernels, join_grads(): pl.pallas_call(final_kernel, grid=(rows // block,), in_specs=[SMEM_SPEC,...  6.31 us
    pallas_call x1, Pallas kernels, run_head(): pl.pallas_call(head_kernel, grid=(CHUNKS,), in_specs=[SMEM_SPEC, pl.Block...  5.97 us
  transfers between devices with their start and end apart: 9, of which 6 were waited for; matrix products, arithmetic and copies ran while one was open for 8% of the time, Pallas kernels for 8%

profile of v2, /device:TPU:16, one launch (start us, length us, event | category | flops | bytes accessed | tf_op | source)
XLA Modules:
  0.0 185.4 jit_solution(1137415863919478809)
XLA Ops:
  0.6 4.6 %shard_map.93 = bf16[64,16,1024]{2,1,0:T(8,128)(2,1)} custom-call(s32[1]{0:T(128)} %bitcast.mine_ref, bf16[1024,2,8,128]{3,2,1,0:T(8,128)(2,1)} %bitcast.32), custom_call_target="tpu_custom_call" | custom-call | bytes 6291456 | tf_op jit(solution)/shard_map/pallas_call | solution.py:98
  5.2 12.9 %all-to-all-start = ((bf16[64,16,1024]{2,1,0:T(8,128)(2,1)}), bf16[64,16,1024]{2,1,0:T(8,128)(2,1)}, u32[]{:S(2)}, u32[]{:S(2)}) async-start(bf16[64,16,1024]{2,1,0:T(8,128)(2,1)} %shard_map.93), calls=%async_computation | async-start | bytes 4194304 | tf_op jit(solution)/shard_map/all_to_all | solution.py:434
  18.2 0.0 copy-start.3
  18.2 4.6 %shard_map.92.own_ref = bf16[2,512,1024]{2,1,0:T(8,128)(2,1)} custom-call(s32[1]{0:T(128)} %bitcast.mine_ref, bf16[1024,2,8,128]{3,2,1,0:T(8,128)(2,1)} %bitcast.33), custom_call_target="tpu_custom_call" | custom-call | bytes 6291456 | tf_op jit(solution)/shard_map/pallas_call | solution.py:98
  22.8 0.0 copy-done.3
  22.8 0.0 copy-start.6
  22.8 0.0 copy-start
  22.8 0.8 copy.18
  23.6 1.5 copy.19.weights_ref
  25.1 0.0 copy-done.6
  25.2 0.7 broadcast_in_dim.6.out_weight_ref
  25.9 43.3 %all-to-all-done.other_ref = bf16[64,16,1024]{2,1,0:T(8,128)(2,1)} async-done(((bf16[64,16,1024]{2,1,0:T(8,128)(2,1)}), bf16[64,16,1024]{2,1,0:T(8,128)(2,1)}, u32[]{:S(2)}, u32[]{:S(2)}) %all-to-all-start) | async-done | bytes 2097184 | tf_op jit(solution)/shard_map/all_to_all | solution.py:434
  69.2 0.0 copy-done
  69.2 2.9 %shard_map.94 = bf16[512,1024]{1,0:T(8,128)(2,1)S(1)} custom-call(s32[1]{0:T(128)} %bitcast.mine_ref, bf16[2,512,1024]{2,1,0:T(8,128)(2,1)S(1)} %copy-done, bf16[64,16,1024]{2,1,0:T(8,128)(2,1)} %all-to-all-done.other_ref, bf16[2,512,512]{2,1,0:T(8,128)(2,1)S(1)} %copy.19.weights_ref), custom_call_target="tpu_custom_call" | custom-call | flops 1073741824 | bytes 8388608 | tf_op jit(solution)/shard_map/pallas_call | solution.py:170
  72.0 19.1 %all_to_all.25 = bf16[16,32,1024]{2,1,0:T(8,128)(2,1)S(1)} all-to-all(bf16[16,32,1024]{2,1,0:T(8,128)(2,1)S(1)} %bitcast.31), channel_id=1, replica_groups={{0,1,2,3,4,5,6,7,8,9,10,11,12,13,14,15},{16,17,18,19,20,21,22,23,24,25,..., dimensions={0} | all-to-all | bytes 2097152 | tf_op jit(solution)/shard_map/all_to_all | solution.py:434
  91.2 0.2 reduce_sum.24
  91.4 12.5 %all_to_all.26 = bf16[4,32,1024]{2,1,0:T(8,128)(2,1)S(1)} all-to-all(bf16[4,32,1024]{2,1,0:T(8,128)(2,1)S(1)} %broadcast_in_dim.7), channel_id=1, replica_groups={{0,16,32,48},{1,17,33,49},{2,18,34,50},{3,19,35,51},{4,20,36,52},{5,21,..., dimensions={0} | all-to-all | bytes 524288 | tf_op jit(solution)/shard_map/all_to_all | solution.py:434
  103.9 0.1 broadcast_in_dim.8
  104.0 16.5 %all_to_all.27 = bf16[16,32,1024]{2,1,0:T(8,128)(2,1)} all-to-all(bf16[16,32,1024]{2,1,0:T(8,128)(2,1)S(1)} %broadcast_in_dim.8), channel_id=1, replica_groups={{0,1,2,3,4,5,6,7,8,9,10,11,12,13,14,15},{16,17,18,19,20,21,22,23,24,25,..., dimensions={0} | all-to-all | bytes 2097152 | tf_op jit(solution)/shard_map/all_to_all | solution.py:434
  120.5 6.0 %shard_map.95 = (f32[1,1024]{1,0:T(1,128)}, f32[512,256]{1,0:T(8,128)}, f32[256,1]{1,0:T(8,128)}, bf16[512,1024]{1,0:T(8,128)(2,1)}, bf16[64,16,1024]{2,1,0:T(8,128)(2,1)}) custom-call(s32[1]{0:T(128)} %bitcast.mine_ref, bf16[512,1024]{1,0:T(8,128)(2,1)} %bitcast.39, bf16[512,256]{1,0:T(8,128)(2,1)} %second_ref.1, bf16[256,512]{1,0:T(8,128)(2,1)} %bitcast.40, ...), custom_call_target="tpu_custom_call" | custom-call | flops 1073741824 | bytes 12582912 | tf_op jit(solution)/shard_map/pallas_call | solution.py:274
  126.5 5.8 %all-to-all-start.4 = ((bf16[64,16,1024]{2,1,0:T(8,128)(2,1)}), bf16[64,16,1024]{2,1,0:T(8,128)(2,1)S(1)}, u32[]{:S(2)}, u32[]{:S(2)}) async-start(bf16[64,16,1024]{2,1,0:T(8,128)(2,1)} %get-tuple-element.30), calls=%async_computation.4 | async-start | bytes 4194304 | tf_op jit(solution)/shard_map/all_to_all | solution.py:434
  132.3 4.4 %shard_map.96 = f32[2,512,512]{2,1,0:T(8,128)} custom-call(s32[1]{0:T(128)} %bitcast.mine_ref, bf16[2,512,1024]{2,1,0:T(8,128)(2,1)} %shard_map.92.own_ref, bf16[64,16,1024]{2,1,0:T(8,128)(2,1)} %all-to-all-done.other_ref, bf16[512,1024]{1,0:T(8,128)(2,1)} %get-tuple-element.28.grad_hidden_ref), custom_call_target="tpu_custom_call" | custom-call | flops 1073741824 | bytes 8388608 | tf_op jit(solution)/shard_map/pallas_call | solution.py:198
  136.6 1.8 constant_dynamic-slice_fusion.1
  138.4 0.0 copy-start.4
  138.4 1.0 copy.24
  139.5 0.0 collective-permute-start
  139.5 0.1 copy-done.4
  139.6 0.5 collective-permute-start.1
  140.1 0.0 copy-start.5
  140.1 2.5 %collective-permute-done.1 = f32[256,256]{1,0:T(8,128)} collective-permute-done((f32[256,256]{1,0:T(8,128)S(1)}, f32[256,256]{1,0:T(8,128)}, u32[]{:S(2)}, u32[]{:S(2)}) %collective-permute-start.1) | collective-permute-done | bytes 262176 | tf_op jit(solution)/shard_map/ppermute | solution.py:451
  142.6 1.1 bitcast_add_fusion.2
  143.7 0.0 collective-permute-done
  143.7 1.4 bitcast_add_fusion
  145.2 0.0 copy-start.1
  145.2 1.0 copy-done.1
  146.1 0.7 fusion
  146.9 0.6 collective-permute-start.4
  147.5 2.9 %collective-permute-start.3 = (bf16[2,16,8,512]{3,2,1,0:T(8,128)(2,1)}, bf16[2,16,8,512]{3,2,1,0:T(8,128)(2,1)}, u32[]{:S(2)}, u32[]{:S(2)}) collective-permute-start(bf16[2,16,8,512]{3,2,1,0:T(8,128)(2,1)} %fusion), channel_id=1, source_target_pairs={{0,128},{128,0},{64,192},{192,64},{1,129},{129,1},{65,193},{193,65... | collective-permute-start | bytes 786440 | tf_op jit(solution)/shard_map/ppermute | solution.py:451
  150.4 0.0 copy-done.5
  150.4 0.1 reduce.2
  150.5 0.3 collective-permute-start.2
  150.8 1.1 collective-permute-done.2
  151.9 0.0 copy-start.2
  151.9 6.7 %shard_map.97.back_ref = f32[1024,8,128]{2,1,0:T(8,128)} custom-call(s32[1]{0:T(128)} %bitcast.mine_ref, bf16[2,512,512]{2,1,0:T(8,128)(2,1)} %bitcast.36, bf16[512,1024]{1,0:T(8,128)(2,1)} %get-tuple-element.28.grad_hidden_ref, bf16[64,16,1024]{2,1,0:T(8,128)(2,1)} %all-to-all-done.other_ref), custom_call_target="tpu_custom_call" | custom-call | flops 1073741824 | bytes 6291456 | tf_op jit(solution)/shard_map/pallas_call | solution.py:388
  158.6 4.3 %collective-permute-done.4 = f32[256,256]{1,0:T(8,128)} collective-permute-done((f32[256,256]{1,0:T(8,128)S(1)}, f32[256,256]{1,0:T(8,128)}, u32[]{:S(2)}, u32[]{:S(2)}) %collective-permute-start.4) | collective-permute-done | bytes 262176 | tf_op jit(solution)/shard_map/ppermute | solution.py:451
  162.9 1.7 add.51
  164.6 0.0 collective-permute-start.5
  164.6 0.0 collective-permute-start.6
  164.6 7.9 %collective-permute-done.6 = f32[256]{0:T(256)S(1)} collective-permute-done((f32[256]{0:T(256)S(1)}, f32[256]{0:T(256)S(1)}, u32[]{:S(2)}, u32[]{:S(2)}) %collective-permute-start.6) | collective-permute-done | bytes 1056 | tf_op jit(solution)/shard_map/ppermute | solution.py:451
  172.6 0.6 add.52
  173.1 0.0 collective-permute-done.3
  173.1 0.0 copy-done.2
  173.1 1.8 bitcast_add_fusion.1
  175.0 0.0 collective-permute-done.5
  175.0 1.0 select_bitcast_fusion.1
  176.0 0.8 pad_maximum_fusion
  176.8 2.3 %all-to-all-done.4.arrived_ref = bf16[64,16,1024]{2,1,0:T(8,128)(2,1)S(1)} async-done(((bf16[64,16,1024]{2,1,0:T(8,128)(2,1)}), bf16[64,16,1024]{2,1,0:T(8,128)(2,1)S(1)}, u32[]{:S(2)}, u32[]{:S(2)}) %all-to-all-start.4) | async-done | bytes 2097184 | tf_op jit(solution)/shard_map/all_to_all | solution.py:434
  179.0 6.3 %shard_map.98 = f32[1024,2,8,128]{3,2,1,0:T(8,128)} custom-call(s32[1]{0:T(128)} %bitcast.mine_ref, f32[1024,8,128]{2,1,0:T(8,128)} %shard_map.97.back_ref, bf16[64,16,1024]{2,1,0:T(8,128)(2,1)S(1)} %all-to-all-done.4.arrived_ref), custom_call_target="tpu_custom_call" | custom-call | bytes 14680064 | tf_op jit(solution)/shard_map/pallas_call | solution.py:409
  (4 shorter events, 0.1 us)
Async XLA Ops:
  5.2 63.9 %all-to-all-start = ((bf16[64,16,1024]{2,1,0:T(8,128)(2,1)}), bf16[64,16,1024]{2,1,0:T(8,128)(2,1)}, u32[]{:S(2)}, u32[]{:S(2)}) async-start(bf16[64,16,1024]{2,1,0:T(8,128)(2,1)} %shard_map.93), calls=%async_computation | async-start | bytes 4194304 | tf_op jit(solution)/shard_map/all_to_all | solution.py:434
  18.2 4.6 %copy-start.3 = (bf16[512,256]{1,0:T(8,128)(2,1)S(1)}, bf16[512,256]{1,0:T(8,128)(2,1)}, u32[]{:S(2)}) copy-start(bf16[512,256]{1,0:T(8,128)(2,1)} %second_ref.1) | copy-start | bytes 786436
  22.8 2.4 %copy-start.6 = (f32[256]{0:T(256)S(1)}, f32[256]{0:T(256)}, u32[]{:S(2)}) copy-start(f32[256]{0:T(256)} %param.8) | copy-start | bytes 3076
  22.8 46.4 %copy-start = (bf16[2,512,1024]{2,1,0:T(8,128)(2,1)S(1)}, bf16[2,512,1024]{2,1,0:T(8,128)(2,1)}, u32[]{:S(2)}) copy-start(bf16[2,512,1024]{2,1,0:T(8,128)(2,1)} %shard_map.92.own_ref) | copy-start | bytes 6291460
  126.5 52.6 %all-to-all-start.4 = ((bf16[64,16,1024]{2,1,0:T(8,128)(2,1)}), bf16[64,16,1024]{2,1,0:T(8,128)(2,1)S(1)}, u32[]{:S(2)}, u32[]{:S(2)}) async-start(bf16[64,16,1024]{2,1,0:T(8,128)(2,1)} %get-tuple-element.30), calls=%async_computation.4 | async-start | bytes 4194304 | tf_op jit(solution)/shard_map/all_to_all | solution.py:434
  138.4 1.2 copy-start.4
  139.5 4.2 %collective-permute-start = (f32[2,2,16,8,512]{4,3,2,0,1:T(8,128)}, f32[2,2,16,8,512]{4,3,2,0,1:T(8,128)}, u32[]{:S(2)}, u32[]{:S(2)}) collective-permute-start(f32[2,2,16,8,512]{4,3,2,0,1:T(8,128)} %bitcast.30), channel_id=1, source_target_pairs={{0,64},{64,0},{128,192},{192,128},{1,65},{65,1},{129,193},{193,129... | collective-permute-start | bytes 3145736 | tf_op jit(solution)/shard_map/ppermute | solution.py:451
  139.6 3.0 %collective-permute-start.1 = (f32[256,256]{1,0:T(8,128)S(1)}, f32[256,256]{1,0:T(8,128)}, u32[]{:S(2)}, u32[]{:S(2)}) collective-permute-start(f32[256,256]{1,0:T(8,128)S(1)} %dynamic-slice_bitcast_fusion), channel_id=1, source_target_pairs={{0,64},{64,0},{128,192},{192,128},{1,65},{65,1},{129,193},{193,129... | collective-permute-start | bytes 786440 | tf_op jit(solution)/shard_map/ppermute | solution.py:451
  140.1 10.3 %copy-start.5 = (f32[256,1]{1,0:T(8,128)S(1)}, f32[256,1]{1,0:T(8,128)}, u32[]{:S(2)}) copy-start(f32[256,1]{1,0:T(8,128)} %get-tuple-element.27) | copy-start | bytes 3076
  145.2 1.0 copy-start.1
  146.9 16.1 %collective-permute-start.4 = (f32[256,256]{1,0:T(8,128)S(1)}, f32[256,256]{1,0:T(8,128)}, u32[]{:S(2)}, u32[]{:S(2)}) collective-permute-start(f32[256,256]{1,0:T(8,128)S(1)} %bitcast_add_fusion.2), channel_id=1, source_target_pairs={{0,128},{128,0},{64,192},{192,64},{1,129},{129,1},{65,193},{193,65... | collective-permute-start | bytes 786440 | tf_op jit(solution)/shard_map/ppermute | solution.py:451
  147.5 25.7 %collective-permute-start.3 = (bf16[2,16,8,512]{3,2,1,0:T(8,128)(2,1)}, bf16[2,16,8,512]{3,2,1,0:T(8,128)(2,1)}, u32[]{:S(2)}, u32[]{:S(2)}) collective-permute-start(bf16[2,16,8,512]{3,2,1,0:T(8,128)(2,1)} %fusion), channel_id=1, source_target_pairs={{0,128},{128,0},{64,192},{192,64},{1,129},{129,1},{65,193},{193,65... | collective-permute-start | bytes 786440 | tf_op jit(solution)/shard_map/ppermute | solution.py:451
  150.5 1.4 collective-permute-start.2
  151.9 21.2 %copy-start.2 = (f32[2,2,16,8,512]{4,3,2,0,1:T(8,128)S(1)}, f32[2,2,16,8,512]{4,3,2,0,1:T(8,128)}, u32[]{:S(2)}) copy-start(f32[2,2,16,8,512]{4,3,2,0,1:T(8,128)} %copy-done.1) | copy-start | bytes 3145732
  164.6 10.3 %collective-permute-start.5 = (f32[256,256]{1,0:T(8,128)}, f32[256,256]{1,0:T(8,128)S(1)}, u32[]{:S(2)}, u32[]{:S(2)}) collective-permute-start(f32[256,256]{1,0:T(8,128)} %add.51), channel_id=1, source_target_pairs={{0,64},{64,0},{128,192},{192,128},{1,65},{65,1},{129,193},{193,129... | collective-permute-start | bytes 786440 | tf_op jit(solution)/shard_map/ppermute | solution.py:451
  164.6 7.9 %collective-permute-start.6 = (f32[256]{0:T(256)S(1)}, f32[256]{0:T(256)S(1)}, u32[]{:S(2)}, u32[]{:S(2)}) collective-permute-start(f32[256]{0:T(256)S(1)} %add.48), channel_id=1, source_target_pairs={{0,128},{128,0},{64,192},{192,64},{1,129},{129,1},{65,193},{193,65... | collective-permute-start | bytes 3080 | tf_op jit(solution)/shard_map/ppermute | solution.py:451

commit v3 on v2

--- a/solution.py
+++ b/solution.py
@@ -9,6 +9,7 @@
 LANES = 128
 TURN = 512
 CHUNKS = 2
+STORE = 256
 MIB = 1024 * 1024
 CORE_PAIRS = [(0, 1), (1, 0), (2, 3), (3, 2)]
 FAR_PAIRS = [(0, 2), (2, 0), (1, 3), (3, 1)]
@@ -313,9 +314,9 @@
 
 
 def turn_back(rows, latent, lanes, turned_ref, planes_ref):
+    turned = jnp.swapaxes(turned_ref[...].reshape(lanes, latent, rows), 0, 1)
     for k in range(latent):
-        plane = turned_ref[pl.ds(k, lanes, stride=latent), :]
-        planes_ref[pl.ds(k, rows, stride=latent), :] = plane.T
+        planes_ref[pl.ds(k, rows, stride=latent), :] = turned[k].T
     return planes_ref[...].reshape(rows, latent, lanes)
 
 
@@ -362,15 +363,59 @@
         )
 
 
-def final_kernel(mine_ref, back_ref, arrived_ref, grads_ref, *scratch):
-    for piece in pieces(back_ref.shape[0]):
+def groups_of(rows):
+    size = min(rows, STORE)
+    return [pl.ds(at, size) for at in range(0, rows, size)]
+
+
+def final_kernel(
+    mine_ref,
+    back_ref,
+    arrived_ref,
+    grads_ref,
+    back_held,
+    arrived_held,
+    ready_ref,
+    back_sems,
+    arrived_sems,
+    store_sems,
+    *scratch,
+):
+    rows = back_held.shape[0]
+    each = len(pieces(rows)) // len(groups_of(rows))
+    arrivals, loads, stores = [], [], []
+    for at, piece in enumerate(pieces(rows)):
+        if at % each == 0:
+            group = groups_of(rows)[at // each]
+            arrivals.append(
+                pltpu.make_async_copy(
+                    arrived_ref.at[:, :, group],
+                    arrived_held.at[:, :, group],
+                    arrived_sems.at[at // each],
+                )
+            )
+            arrivals[-1].start()
+        loads.append(
+            pltpu.make_async_copy(back_ref.at[piece], back_held.at[piece], back_sems.at[at])
+        )
+        loads[-1].start()
+    for at, piece in enumerate(pieces(rows)):
+        if at % each == 0:
+            arrivals[at // each].wait()
+        loads[at].wait()
         final_part(
             mine_ref,
-            back_ref.at[piece],
-            arrived_ref.at[:, :, piece],
-            grads_ref.at[piece],
+            back_held.at[piece],
+            arrived_held.at[:, :, piece],
+            ready_ref.at[piece],
             *scratch,
         )
+        stores.append(
+            pltpu.make_async_copy(ready_ref.at[piece], grads_ref.at[piece], store_sems.at[at])
+        )
+        stores[-1].start()
+    for store in stores:
+        store.wait()
 
 
 def turn_scratch(block, latent, lanes):
@@ -402,21 +447,27 @@
     )(mine, weights, grad_hidden, other)
 
 
+ANY_SPEC = pl.BlockSpec(memory_space=pl.ANY)
+
+
 def join_grads(mine, back, arrived):
     rows, latent, lanes = back.shape
-    owners, wide, _ = arrived.shape
-    block = min(rows, TURN)
+    shape = (rows, 2, latent, lanes)
+    count = len(pieces(rows))
     return pl.pallas_call(
         final_kernel,
-        grid=(rows // block,),
-        in_specs=[
-            SMEM_SPEC,
-            pl.BlockSpec((block, latent, lanes), lambda at: (at, 0, 0)),
-            pl.BlockSpec((owners, wide, block), lambda at: (0, 0, at)),
-        ],
-        out_specs=pl.BlockSpec((block, 2, latent, lanes), lambda at: (at, 0, 0, 0)),
-        out_shape=jax.ShapeDtypeStruct((rows, 2, latent, lanes), jnp.float32),
-        scratch_shapes=turn_scratch(block, latent, lanes),
+        in_specs=[SMEM_SPEC, ANY_SPEC, ANY_SPEC],
+        out_specs=ANY_SPEC,
+        out_shape=jax.ShapeDtypeStruct(shape, jnp.float32),
+        scratch_shapes=[
+            pltpu.VMEM(back.shape, jnp.float32),
+            pltpu.VMEM(arrived.shape, jnp.bfloat16),
+            pltpu.VMEM(shape, jnp.float32),
+            pltpu.SemaphoreType.DMA((count,)),
+            pltpu.SemaphoreType.DMA((len(groups_of(rows)),)),
+            pltpu.SemaphoreType.DMA((count,)),
+        ]
+        + turn_scratch(rows, latent, lanes),
         compiler_params=params(48),
         cost_estimate=cost(0, back.size * 14),
     )(mine, back, arrived)

time: 186 us -> 185 us (level)
  no operation moved by 1% of the time
where the time goes in v3:
time: 185 us; the launch traced here: 184 us
  waiting for transfers between devices  61.6 us (33%)
  blocking collectives  48.1 us (26%)
  Pallas kernels  34.2 us (18%)
  starting transfers between devices  22.9 us (12%)
  other arithmetic  8.75 us (5%)
  local copies, waits for them, and re-layouts  7.89 us (4%)
    all_to_all x3, blocking collectives, exchange(): lax.all_to_all(blocks, 'field', 0, 0, axis_index_groups=groups, tiled=True)  48.1 us
    all_to_all x2, waiting for transfers between devices, exchange(): lax.all_to_all(blocks, 'field', 0, 0, axis_index_groups=groups, tiled=True)  45.5 us
    all_to_all x2, starting transfers between devices, exchange(): lax.all_to_all(blocks, 'field', 0, 0, axis_index_groups=groups, tiled=True)  18.7 us
    ppermute x7, waiting for transfers between devices, swap(): return lax.ppermute(value, 'batch', pairs)  16.1 us
    pallas_call x2, Pallas kernels, turn_call(): pl.pallas_call(kernel, grid=(rows // block,), in_specs=[SMEM_SPEC, pl.Blo...  9.21 us
    pallas_call x1, Pallas kernels, turn_own_grads(): pl.pallas_call(own_back_kernel, grid=(rows // block,), in_specs=[SMEM_SPE...  6.56 us
    pallas_call x1, Pallas kernels, run_head(): pl.pallas_call(head_kernel, grid=(CHUNKS,), in_specs=[SMEM_SPEC, pl.Block...  5.97 us
    pallas_call x1, Pallas kernels, join_grads(): pl.pallas_call(final_kernel, in_specs=[SMEM_SPEC, ANY_SPEC, ANY_SPEC], ou...  5.17 us
  transfers between devices with their start and end apart: 9, of which 6 were waited for; matrix products, arithmetic and copies ran while one was open for 8% of the time, Pallas kernels for 8%

profile of v3, /device:TPU:16, one launch (start us, length us, event | category | flops | bytes accessed | tf_op | source)
XLA Modules:
  0.0 184.4 jit_solution(4953378473170513699)
XLA Ops:
  0.6 4.6 %shard_map.93 = bf16[64,16,1024]{2,1,0:T(8,128)(2,1)} custom-call(s32[1]{0:T(128)} %bitcast.mine_ref, bf16[1024,2,8,128]{3,2,1,0:T(8,128)(2,1)} %bitcast.32), custom_call_target="tpu_custom_call" | custom-call | bytes 6291456 | tf_op jit(solution)/shard_map/pallas_call | solution.py:99
  5.2 12.9 %all-to-all-start = ((bf16[64,16,1024]{2,1,0:T(8,128)(2,1)}), bf16[64,16,1024]{2,1,0:T(8,128)(2,1)}, u32[]{:S(2)}, u32[]{:S(2)}) async-start(bf16[64,16,1024]{2,1,0:T(8,128)(2,1)} %shard_map.93), calls=%async_computation | async-start | bytes 4194304 | tf_op jit(solution)/shard_map/all_to_all | solution.py:485
  18.2 0.0 copy-start.3
  18.2 4.6 %shard_map.92.own_ref = bf16[2,512,1024]{2,1,0:T(8,128)(2,1)} custom-call(s32[1]{0:T(128)} %bitcast.mine_ref, bf16[1024,2,8,128]{3,2,1,0:T(8,128)(2,1)} %bitcast.33), custom_call_target="tpu_custom_call" | custom-call | bytes 6291456 | tf_op jit(solution)/shard_map/pallas_call | solution.py:99
  22.8 0.0 copy-done.3
  22.8 0.0 copy-start.6
  22.8 0.0 copy-start
  22.8 0.8 copy.18
  23.6 1.5 copy.19.weights_ref
  25.1 0.0 copy-done.6
  25.2 0.7 broadcast_in_dim.6.out_weight_ref
  25.9 43.3 %all-to-all-done.other_ref = bf16[64,16,1024]{2,1,0:T(8,128)(2,1)} async-done(((bf16[64,16,1024]{2,1,0:T(8,128)(2,1)}), bf16[64,16,1024]{2,1,0:T(8,128)(2,1)}, u32[]{:S(2)}, u32[]{:S(2)}) %all-to-all-start) | async-done | bytes 2097184 | tf_op jit(solution)/shard_map/all_to_all | solution.py:485
  69.2 0.0 copy-done
  69.2 2.9 %shard_map.94 = bf16[512,1024]{1,0:T(8,128)(2,1)S(1)} custom-call(s32[1]{0:T(128)} %bitcast.mine_ref, bf16[2,512,1024]{2,1,0:T(8,128)(2,1)S(1)} %copy-done, bf16[64,16,1024]{2,1,0:T(8,128)(2,1)} %all-to-all-done.other_ref, bf16[2,512,512]{2,1,0:T(8,128)(2,1)S(1)} %copy.19.weights_ref), custom_call_target="tpu_custom_call" | custom-call | flops 1073741824 | bytes 8388608 | tf_op jit(solution)/shard_map/pallas_call | solution.py:171
  72.0 19.1 %all_to_all.25 = bf16[16,32,1024]{2,1,0:T(8,128)(2,1)S(1)} all-to-all(bf16[16,32,1024]{2,1,0:T(8,128)(2,1)S(1)} %bitcast.31), channel_id=1, replica_groups={{0,1,2,3,4,5,6,7,8,9,10,11,12,13,14,15},{16,17,18,19,20,21,22,23,24,25,..., dimensions={0} | all-to-all | bytes 2097152 | tf_op jit(solution)/shard_map/all_to_all | solution.py:485
  91.2 0.2 reduce_sum.24
  91.4 12.5 %all_to_all.26 = bf16[4,32,1024]{2,1,0:T(8,128)(2,1)S(1)} all-to-all(bf16[4,32,1024]{2,1,0:T(8,128)(2,1)S(1)} %broadcast_in_dim.7), channel_id=1, replica_groups={{0,16,32,48},{1,17,33,49},{2,18,34,50},{3,19,35,51},{4,20,36,52},{5,21,..., dimensions={0} | all-to-all | bytes 524288 | tf_op jit(solution)/shard_map/all_to_all | solution.py:485
  103.9 0.1 broadcast_in_dim.8
  104.0 16.5 %all_to_all.27 = bf16[16,32,1024]{2,1,0:T(8,128)(2,1)} all-to-all(bf16[16,32,1024]{2,1,0:T(8,128)(2,1)S(1)} %broadcast_in_dim.8), channel_id=1, replica_groups={{0,1,2,3,4,5,6,7,8,9,10,11,12,13,14,15},{16,17,18,19,20,21,22,23,24,25,..., dimensions={0} | all-to-all | bytes 2097152 | tf_op jit(solution)/shard_map/all_to_all | solution.py:485
  120.5 6.0 %shard_map.95 = (f32[1,1024]{1,0:T(1,128)}, f32[512,256]{1,0:T(8,128)}, f32[256,1]{1,0:T(8,128)}, bf16[512,1024]{1,0:T(8,128)(2,1)}, bf16[64,16,1024]{2,1,0:T(8,128)(2,1)}) custom-call(s32[1]{0:T(128)} %bitcast.mine_ref, bf16[512,1024]{1,0:T(8,128)(2,1)} %bitcast.39, bf16[512,256]{1,0:T(8,128)(2,1)} %second_ref.1, bf16[256,512]{1,0:T(8,128)(2,1)} %bitcast.40, ...), custom_call_target="tpu_custom_call" | custom-call | flops 1073741824 | bytes 12582912 | tf_op jit(solution)/shard_map/pallas_call | solution.py:275
  126.5 5.8 %all-to-all-start.4 = ((bf16[64,16,1024]{2,1,0:T(8,128)(2,1)}), bf16[64,16,1024]{2,1,0:T(8,128)(2,1)S(1)}, u32[]{:S(2)}, u32[]{:S(2)}) async-start(bf16[64,16,1024]{2,1,0:T(8,128)(2,1)} %get-tuple-element.30), calls=%async_computation.4 | async-start | bytes 4194304 | tf_op jit(solution)/shard_map/all_to_all | solution.py:485
  132.3 4.4 %shard_map.96 = f32[2,512,512]{2,1,0:T(8,128)} custom-call(s32[1]{0:T(128)} %bitcast.mine_ref, bf16[2,512,1024]{2,1,0:T(8,128)(2,1)} %shard_map.92.own_ref, bf16[64,16,1024]{2,1,0:T(8,128)(2,1)} %all-to-all-done.other_ref, bf16[512,1024]{1,0:T(8,128)(2,1)} %get-tuple-element.28.grad_hidden_ref), custom_call_target="tpu_custom_call" | custom-call | flops 1073741824 | bytes 8388608 | tf_op jit(solution)/shard_map/pallas_call | solution.py:199
  136.6 1.8 constant_dynamic-slice_fusion.1
  138.4 0.0 copy-start.4
  138.4 1.0 copy.24
  139.5 0.0 collective-permute-start
  139.5 0.1 copy-done.4
  139.6 0.5 collective-permute-start.1
  140.1 0.0 copy-start.5
  140.1 2.5 %collective-permute-done.1 = f32[256,256]{1,0:T(8,128)} collective-permute-done((f32[256,256]{1,0:T(8,128)S(1)}, f32[256,256]{1,0:T(8,128)}, u32[]{:S(2)}, u32[]{:S(2)}) %collective-permute-start.1) | collective-permute-done | bytes 262176 | tf_op jit(solution)/shard_map/ppermute | solution.py:502
  142.6 1.1 bitcast_add_fusion.2
  143.7 0.0 collective-permute-done
  143.7 1.4 bitcast_add_fusion
  145.2 0.0 copy-start.1
  145.2 1.0 copy-done.1
  146.1 0.7 fusion
  146.9 0.6 collective-permute-start.4
  147.5 2.9 %collective-permute-start.3 = (bf16[2,16,8,512]{3,2,1,0:T(8,128)(2,1)}, bf16[2,16,8,512]{3,2,1,0:T(8,128)(2,1)}, u32[]{:S(2)}, u32[]{:S(2)}) collective-permute-start(bf16[2,16,8,512]{3,2,1,0:T(8,128)(2,1)} %fusion), channel_id=1, source_target_pairs={{0,128},{128,0},{64,192},{192,64},{1,129},{129,1},{65,193},{193,65... | collective-permute-start | bytes 786440 | tf_op jit(solution)/shard_map/ppermute | solution.py:502
  150.4 0.0 copy-done.5
  150.4 0.1 reduce.2
  150.5 0.3 collective-permute-start.2
  150.8 1.1 collective-permute-done.2
  151.9 0.0 copy-start.2
  151.9 6.6 %shard_map.97.back_ref = f32[1024,8,128]{2,1,0:T(8,128)} custom-call(s32[1]{0:T(128)} %bitcast.mine_ref, bf16[2,512,512]{2,1,0:T(8,128)(2,1)} %bitcast.36, bf16[512,1024]{1,0:T(8,128)(2,1)} %get-tuple-element.28.grad_hidden_ref, bf16[64,16,1024]{2,1,0:T(8,128)(2,1)} %all-to-all-done.other_ref), custom_call_target="tpu_custom_call" | custom-call | flops 1073741824 | bytes 6291456 | tf_op jit(solution)/shard_map/pallas_call | solution.py:433
  158.5 4.5 %collective-permute-done.4 = f32[256,256]{1,0:T(8,128)} collective-permute-done((f32[256,256]{1,0:T(8,128)S(1)}, f32[256,256]{1,0:T(8,128)}, u32[]{:S(2)}, u32[]{:S(2)}) %collective-permute-start.4) | collective-permute-done | bytes 262176 | tf_op jit(solution)/shard_map/ppermute | solution.py:502
  162.9 1.7 add.51
  164.6 0.0 collective-permute-start.5
  164.6 0.0 collective-permute-start.6
  164.6 7.9 %collective-permute-done.6 = f32[256]{0:T(256)S(1)} collective-permute-done((f32[256]{0:T(256)S(1)}, f32[256]{0:T(256)S(1)}, u32[]{:S(2)}, u32[]{:S(2)}) %collective-permute-start.6) | collective-permute-done | bytes 1056 | tf_op jit(solution)/shard_map/ppermute | solution.py:502
  172.6 0.6 add.52
  173.1 0.0 collective-permute-done.3
  173.1 0.0 copy-done.2
  173.1 1.8 bitcast_add_fusion.1
  175.0 0.0 collective-permute-done.5
  175.0 1.0 select_bitcast_fusion.1
  176.0 0.8 pad_maximum_fusion
  176.8 2.3 %all-to-all-done.4.arrived_ref = bf16[64,16,1024]{2,1,0:T(8,128)(2,1)S(1)} async-done(((bf16[64,16,1024]{2,1,0:T(8,128)(2,1)}), bf16[64,16,1024]{2,1,0:T(8,128)(2,1)S(1)}, u32[]{:S(2)}, u32[]{:S(2)}) %all-to-all-start.4) | async-done | bytes 2097184 | tf_op jit(solution)/shard_map/all_to_all | solution.py:485
  179.0 5.2 %shard_map.98 = f32[1024,2,8,128]{3,2,1,0:T(8,128)} custom-call(s32[1]{0:T(128)} %bitcast.mine_ref, f32[1024,8,128]{2,1,0:T(8,128)} %shard_map.97.back_ref, bf16[64,16,1024]{2,1,0:T(8,128)(2,1)S(1)} %all-to-all-done.4.arrived_ref), custom_call_target="tpu_custom_call" | custom-call | bytes 14680064 | tf_op jit(solution)/shard_map/pallas_call | solution.py:457
  (4 shorter events, 0.1 us)
Async XLA Ops:
  5.2 63.9 %all-to-all-start = ((bf16[64,16,1024]{2,1,0:T(8,128)(2,1)}), bf16[64,16,1024]{2,1,0:T(8,128)(2,1)}, u32[]{:S(2)}, u32[]{:S(2)}) async-start(bf16[64,16,1024]{2,1,0:T(8,128)(2,1)} %shard_map.93), calls=%async_computation | async-start | bytes 4194304 | tf_op jit(solution)/shard_map/all_to_all | solution.py:485
  18.2 4.6 %copy-start.3 = (bf16[512,256]{1,0:T(8,128)(2,1)S(1)}, bf16[512,256]{1,0:T(8,128)(2,1)}, u32[]{:S(2)}) copy-start(bf16[512,256]{1,0:T(8,128)(2,1)} %second_ref.1) | copy-start | bytes 786436
  22.8 2.4 %copy-start.6 = (f32[256]{0:T(256)S(1)}, f32[256]{0:T(256)}, u32[]{:S(2)}) copy-start(f32[256]{0:T(256)} %param.8) | copy-start | bytes 3076
  22.8 46.4 %copy-start = (bf16[2,512,1024]{2,1,0:T(8,128)(2,1)S(1)}, bf16[2,512,1024]{2,1,0:T(8,128)(2,1)}, u32[]{:S(2)}) copy-start(bf16[2,512,1024]{2,1,0:T(8,128)(2,1)} %shard_map.92.own_ref) | copy-start | bytes 6291460
  126.5 52.6 %all-to-all-start.4 = ((bf16[64,16,1024]{2,1,0:T(8,128)(2,1)}), bf16[64,16,1024]{2,1,0:T(8,128)(2,1)S(1)}, u32[]{:S(2)}, u32[]{:S(2)}) async-start(bf16[64,16,1024]{2,1,0:T(8,128)(2,1)} %get-tuple-element.30), calls=%async_computation.4 | async-start | bytes 4194304 | tf_op jit(solution)/shard_map/all_to_all | solution.py:485
  138.4 1.2 copy-start.4
  139.5 4.2 %collective-permute-start = (f32[2,2,16,8,512]{4,3,2,0,1:T(8,128)}, f32[2,2,16,8,512]{4,3,2,0,1:T(8,128)}, u32[]{:S(2)}, u32[]{:S(2)}) collective-permute-start(f32[2,2,16,8,512]{4,3,2,0,1:T(8,128)} %bitcast.30), channel_id=1, source_target_pairs={{0,64},{64,0},{128,192},{192,128},{1,65},{65,1},{129,193},{193,129... | collective-permute-start | bytes 3145736 | tf_op jit(solution)/shard_map/ppermute | solution.py:502
  139.6 3.0 %collective-permute-start.1 = (f32[256,256]{1,0:T(8,128)S(1)}, f32[256,256]{1,0:T(8,128)}, u32[]{:S(2)}, u32[]{:S(2)}) collective-permute-start(f32[256,256]{1,0:T(8,128)S(1)} %dynamic-slice_bitcast_fusion), channel_id=1, source_target_pairs={{0,64},{64,0},{128,192},{192,128},{1,65},{65,1},{129,193},{193,129... | collective-permute-start | bytes 786440 | tf_op jit(solution)/shard_map/ppermute | solution.py:502
  140.1 10.3 %copy-start.5 = (f32[256,1]{1,0:T(8,128)S(1)}, f32[256,1]{1,0:T(8,128)}, u32[]{:S(2)}) copy-start(f32[256,1]{1,0:T(8,128)} %get-tuple-element.27) | copy-start | bytes 3076
  145.2 1.0 copy-start.1
  146.9 16.1 %collective-permute-start.4 = (f32[256,256]{1,0:T(8,128)S(1)}, f32[256,256]{1,0:T(8,128)}, u32[]{:S(2)}, u32[]{:S(2)}) collective-permute-start(f32[256,256]{1,0:T(8,128)S(1)} %bitcast_add_fusion.2), channel_id=1, source_target_pairs={{0,128},{128,0},{64,192},{192,64},{1,129},{129,1},{65,193},{193,65... | collective-permute-start | bytes 786440 | tf_op jit(solution)/shard_map/ppermute | solution.py:502
  147.5 25.7 %collective-permute-start.3 = (bf16[2,16,8,512]{3,2,1,0:T(8,128)(2,1)}, bf16[2,16,8,512]{3,2,1,0:T(8,128)(2,1)}, u32[]{:S(2)}, u32[]{:S(2)}) collective-permute-start(bf16[2,16,8,512]{3,2,1,0:T(8,128)(2,1)} %fusion), channel_id=1, source_target_pairs={{0,128},{128,0},{64,192},{192,64},{1,129},{129,1},{65,193},{193,65... | collective-permute-start | bytes 786440 | tf_op jit(solution)/shard_map/ppermute | solution.py:502
  150.5 1.4 collective-permute-start.2
  151.9 21.2 %copy-start.2 = (f32[2,2,16,8,512]{4,3,2,0,1:T(8,128)S(1)}, f32[2,2,16,8,512]{4,3,2,0,1:T(8,128)}, u32[]{:S(2)}) copy-start(f32[2,2,16,8,512]{4,3,2,0,1:T(8,128)} %copy-done.1) | copy-start | bytes 3145732
  164.6 10.3 %collective-permute-start.5 = (f32[256,256]{1,0:T(8,128)}, f32[256,256]{1,0:T(8,128)S(1)}, u32[]{:S(2)}, u32[]{:S(2)}) collective-permute-start(f32[256,256]{1,0:T(8,128)} %add.51), channel_id=1, source_target_pairs={{0,64},{64,0},{128,192},{192,128},{1,65},{65,1},{129,193},{193,129... | collective-permute-start | bytes 786440 | tf_op jit(solution)/shard_map/ppermute | solution.py:502
  164.6 7.9 %collective-permute-start.6 = (f32[256]{0:T(256)S(1)}, f32[256]{0:T(256)S(1)}, u32[]{:S(2)}, u32[]{:S(2)}) collective-permute-start(f32[256]{0:T(256)S(1)} %add.48), channel_id=1, source_target_pairs={{0,128},{128,0},{64,192},{192,64},{1,129},{129,1},{65,193},{193,65... | collective-permute-start | bytes 3080 | tf_op jit(solution)/shard_map/ppermute | solution.py:502
